TPU v7x, 256 devices: a whole 4x4x8 slice. The times are simulated.
256 devices in a mesh: tile: 64 (over x, z, core), lev: 4 (over y).
Axes of the slice: x: 4, y: 4, z: 8, core: 2. Of those that a mesh axis runs over, the one named last changes fastest.
Arguments:
- anomalies: bfloat16 [50, 16, 1152, 384], P(None, 'lev', 'tile'), may hold values from -6 to 6
- lanczos: bfloat16 [100, 16, 1152, 384], P(None, 'lev', 'tile'), may hold values from -6 to 6
- eigen_weight: float32 [100], replicated, may hold values from 0.02 to 0.3
- stencil_index: int32 [6, 49152], P(None, 'tile'), may hold values from 0 to 9215, as said below
- stencil_weight: float32 [6, 49152], P(None, 'tile'), may hold values from 0.05 to 0.35
- member_slot: int32 [50], replicated, may hold values from 0 to 63, as said below
Outputs:
- updated: bfloat16 [50, 16, 1152, 384], P(None, 'lev', 'tile')
- owned: bfloat16 [64, 16, 384, 128], P('tile', 'lev')
Inputs may be any that keep to these rules, and one draw needn't show every extreme that they name: `stencil_index`: positions within a block of 24 x 384. `member_slot`: distinct for distinct members; slot s belongs to tile s.
All inputs are finite; a program needn't handle non-finite values.
Results may differ from a plain program's by a relative error of at most 0.0065.
Values may be sent and summed in bfloat16 or wider, within the bound.
A program may use at most 128 MiB of HBM per device.

v0:
```python
import math

import jax
import jax.numpy as jnp
from jax import lax
from jax.sharding import PartitionSpec as P


def with_halo(block, sides, width):
    for axis, dim in sides:
        count = lax.axis_size(axis)
        forward = [(i, i + 1) for i in range(count - 1)]
        backward = [(target, source) for source, target in forward]
        low = lax.ppermute(
            lax.slice_in_dim(block, block.shape[dim] - width, None, axis=dim), axis, forward
        )
        high = lax.ppermute(lax.slice_in_dim(block, 0, width, axis=dim), axis, backward)
        block = jnp.concatenate([low, block, high], axis=dim)
    return block


def apply_update(flat_x, flat_v, coefficients):
    increment = lax.dot_general(
        coefficients, flat_v, (((0,), (0,)), ((), ())), preferred_element_type=jnp.float32
    )
    return (flat_x - increment).astype(jnp.bfloat16)


def stencil_sums(flat_pad, index_rows, weight_rows):
    points, count = index_rows.shape
    picked = jnp.take(flat_pad, index_rows.reshape(-1), axis=1).reshape(
        flat_pad.shape[0], points, count
    )
    return (picked.astype(jnp.float32) * weight_rows[None]).sum(1)


def shards(anomalies, lanczos, eigen_weight, stencil_index, stencil_weight, member_slot):
    members, levels, rows, cols = anomalies.shape
    vectors = lanczos.shape[0]
    tiles = lax.axis_size("tile")
    total_cells = levels * rows * cols * tiles * lax.axis_size("lev")
    coarse_rows = rows // 3
    coarse_cols = cols // 3
    flat_x = anomalies.reshape(members, -1)
    flat_v = lanczos.reshape(vectors, -1)
    partial_sum = lax.dot_general(
        flat_v, flat_x, (((1,), (1,)), ((), ())), preferred_element_type=jnp.float32
    )
    projection = lax.psum(partial_sum, ("tile", "lev"))
    coefficients = (eigen_weight[:, None] * projection / math.sqrt(total_cells)).astype(
        jnp.bfloat16
    )
    updated = apply_update(flat_x, flat_v, coefficients).reshape(members, levels, rows, cols)
    padded = with_halo(updated, (("tile", 2),), 3)
    flat_pad = padded.reshape(members * levels, -1)
    restricted = stencil_sums(flat_pad, stencil_index, stencil_weight).astype(jnp.bfloat16)
    per_tile = (members + tiles - 1) // tiles
    slot_count = tiles * per_tile
    selector = (member_slot[None, :] == jnp.arange(slot_count, dtype=jnp.int32)[:, None]).astype(
        jnp.bfloat16
    )
    outgoing = jnp.dot(
        selector, restricted.reshape(members, -1), preferred_element_type=jnp.float32
    )
    outgoing = outgoing.astype(jnp.bfloat16).reshape(slot_count, levels, coarse_rows, coarse_cols)
    owned = lax.all_to_all(outgoing, "tile", split_axis=0, concat_axis=2, tiled=True)
    return (updated, owned)


def solution(mesh):
    placed = (
        P(None, "lev", "tile", None),
        P(None, "lev", "tile", None),
        P(),
        P(None, "tile"),
        P(None, "tile"),
        P(),
    )
    return jax.shard_map(
        shards,
        mesh=mesh,
        in_specs=placed,
        out_specs=(P(None, "lev", "tile", None), P("tile", "lev", None, None)),
        check_vma=False,
    )
```

profile of v0, /device:TPU:1, one launch (start us, length us, event | category | flops | bytes accessed | tf_op | source)
XLA Modules:
  0.0 186.9 jit_solution(5968356691390355360)
XLA Ops:
  0.6 5.9 %copy.43 = f32[50,4,18,384]{3,2,1,0:T(8,128)} copy(bf16[50,4,18,384]{3,1,2,0:T(4,128)(2,1)} %param.6) | data formatting | bytes 8294400 | tf_op jit(solution)/shard_map/convert_element_type | solution.py:26
  6.6 4.3 %copy.46 = bf16[100,4,18,384]{3,2,1,0:T(8,128)(2,1)} copy(bf16[100,4,18,384]{3,1,2,0:T(4,128)(2,1)S(1)} %copy-done.1) | data formatting | bytes 11059200 | tf_op args[1]
  10.9 2.1 %fusion.4 = f32[100,50]{0,1:T(8,128)S(1)} fusion(bf16[50,4,18,384]{3,1,2,0:T(4,128)(2,1)S(1)} %copy-done.2, bf16[100,4,18,384]{3,1,2,0:T(4,128)(2,1)S(1)} %copy-done.1), kind=kOutput, calls=%fused_computation.9 | convolution fusion | flops 276480000 | bytes 8314400 | tf_op jit(solution)/shard_map/dot_general | solution.py:46
  13.0 6.9 %reshape.73 = f32[50,27648]{1,0:T(8,128)} reshape(f32[50,4,18,384]{3,2,1,0:T(8,128)} %copy.43) | data formatting | bytes 11059200 | tf_op jit(solution)/shard_map/convert_element_type | solution.py:26
  19.9 8.8 %reshape.68 = bf16[100,27648]{1,0:T(8,128)(2,1)} reshape(bf16[100,4,18,384]{3,2,1,0:T(8,128)(2,1)} %copy.46) | data formatting | bytes 11059200 | tf_op jit(solution)/shard_map/reshape | solution.py:45
  28.7 81.6 %psum.7 = f32[100,50]{0,1:T(8,128)S(1)} all-reduce(f32[100,50]{0,1:T(8,128)S(1)} %fusion.4), channel_id=1, replica_groups=mesh['tile'=64,'lev'=4] {'tile','lev'}, use_global_device_ids=true, to_apply=%region_0.0 | all-reduce | flops 5000 | bytes 40000 | tf_op jit(solution)/shard_map/psum | solution.py:49
  110.2 5.7 %fusion = bf16[50,27648]{1,0:T(8,128)(2,1)S(1)} fusion(f32[50,27648]{1,0:T(8,128)} %reshape.73, bf16[100,27648]{1,0:T(8,128)(2,1)} %reshape.68, f32[100,50]{0,1:T(8,128)S(1)} %psum.7, f32[100]{0:T(128)S(1)} %copy-done.5), kind=kOutput, calls=%fused_computation.2 | convolution fusion | flops 279259808 | bytes 13844400 | tf_op jit(solution)/shard_map/dot_general | solution.py:23
  115.9 3.4 %reshape.69 = bf16[50,4,18,384]{3,2,1,0:T(8,128)(2,1)} reshape(bf16[50,27648]{1,0:T(8,128)(2,1)S(1)} %fusion) | data formatting | bytes 5529600 | tf_op jit(solution)/shard_map/reshape | solution.py:53
  119.3 2.7 %fusion.14 = (bf16[50,4,3,384]{3,2,1,0:T(4,128)(2,1)S(1)}, bf16[50,4,3,384]{3,2,1,0:T(4,128)(2,1)S(1)}) fusion(bf16[50,4,18,384]{3,2,1,0:T(8,128)(2,1)} %reshape.69), kind=kLoop, calls=%fused_computation.21 | loop fusion | bytes 1843200 | tf_op jit(solution)/shard_map/slice | solution.py:15
  122.3 3.4 %collective-permute-start = (bf16[50,4,3,384]{3,1,2,0:T(4,128)(2,1)S(1)}, bf16[50,4,3,384]{3,1,2,0:T(4,128)(2,1)S(1)}, u32[]{:S(2)}, u32[]{:S(2)}) collective-permute-start(bf16[50,4,3,384]{3,1,2,0:T(4,128)(2,1)S(1)} %copy.47), channel_id=1, source_target_pairs={{0,4},{4,8},{8,12},{12,16},{16,20},{20,24},{24,28},{28,32},{32,36}... | collective-permute-start | bytes 1382408 | tf_op jit(solution)/shard_map/ppermute | solution.py:14
  125.9 2.1 %collective-permute-start.1 = (bf16[50,4,3,384]{3,1,2,0:T(4,128)(2,1)S(1)}, bf16[50,4,3,384]{3,1,2,0:T(4,128)(2,1)S(1)}, u32[]{:S(2)}, u32[]{:S(2)}) collective-permute-start(bf16[50,4,3,384]{3,1,2,0:T(4,128)(2,1)S(1)} %copy.48), channel_id=1, source_target_pairs={{4,0},{8,4},{12,8},{16,12},{20,16},{24,20},{28,24},{32,28},{36,32}... | collective-permute-start | bytes 1382408 | tf_op jit(solution)/shard_map/ppermute | solution.py:17
  128.1 3.0 %collective-permute-done = bf16[50,4,3,384]{3,1,2,0:T(4,128)(2,1)S(1)} collective-permute-done((bf16[50,4,3,384]{3,1,2,0:T(4,128)(2,1)S(1)}, bf16[50,4,3,384]{3,1,2,0:T(4,128)(2,1)S(1)}, u32[]{:S(2)}, u32[]{:S(2)}) %collective-permute-start) | collective-permute-done | bytes 460832 | tf_op jit(solution)/shard_map/ppermute | solution.py:14
  131.3 4.4 %collective-permute-done.1 = bf16[50,4,3,384]{3,1,2,0:T(4,128)(2,1)S(1)} collective-permute-done((bf16[50,4,3,384]{3,1,2,0:T(4,128)(2,1)S(1)}, bf16[50,4,3,384]{3,1,2,0:T(4,128)(2,1)S(1)}, u32[]{:S(2)}, u32[]{:S(2)}) %collective-permute-start.1) | collective-permute-done | bytes 460832 | tf_op jit(solution)/shard_map/ppermute | solution.py:17
  135.9 2.8 %pad_maximum_fusion = bf16[50,4,24,384]{3,2,1,0:T(8,128)(2,1)S(1)} fusion(bf16[50,4,3,384]{3,2,1,0:T(4,128)(2,1)S(1)} %copy.50, bf16[50,4,18,384]{3,2,1,0:T(8,128)(2,1)S(1)} %copy-done, bf16[50,4,3,384]{3,2,1,0:T(4,128)(2,1)S(1)} %copy.49), kind=kLoop, calls=%fused_computation.6 | loop fusion | flops 11059200 | bytes 7372800 | tf_op jit(solution)/shard_map/concatenate | solution.py:18
  138.7 2.6 %copy.57 = bf16[25,8,24,384]{3,1,2,0:T(8,128)(2,1)} copy(bf16[25,8,24,384]{3,2,1,0:T(8,128)(2,1)S(1)} %bitcast.21) | data formatting | bytes 7372800
  141.3 6.3 %copy.51 = bf16[200,9216]{0,1:T(8,128)(2,1)} copy(bf16[200,9216]{1,0:T(8,128)(2,1)} %bitcast.22) | data formatting | bytes 7372800 | tf_op jit(solution)/shard_map/reshape | solution.py:55
  147.6 12.8 %gather_fusion = bf16[4608,200]{1,0:T(8,128)(2,1)S(1)} fusion(bf16[200,9216]{0,1:T(8,128)(2,1)} %copy.51, s32[5120]{0:T(1024)S(1)} %pad_clamp_fusion), kind=kCustom, calls=%fused_computation | custom fusion | bytes 3704832 | tf_op jit(solution)/shard_map/jit(_take)/gather | solution.py:31
  160.4 1.6 multiply_reduce_fusion
  162.7 0.5 reshape.72
  163.2 0.9 copy.53
  164.1 7.4 %all-to-all-start = ((bf16[64,4,6,128]{3,1,2,0:T(4,128)(2,1)}), bf16[64,4,6,128]{3,1,2,0:T(4,128)(2,1)S(1)}, u32[]{:S(2)}, u32[]{:S(2)}) async-start(bf16[64,4,6,128]{3,1,2,0:T(4,128)(2,1)} %copy.53), calls=%async_computation | async-start | bytes 786432 | tf_op jit(solution)/shard_map/all_to_all | solution.py:66
  171.5 4.6 %copy.54 = bf16[50,4,18,384]{3,1,2,0:T(4,128)(2,1)} copy(bf16[50,4,18,384]{3,2,1,0:T(8,128)(2,1)} %reshape.69) | data formatting | bytes 5529600
  176.1 10.0 %all-to-all-done = bf16[64,4,6,128]{3,1,2,0:T(4,128)(2,1)S(1)} async-done(((bf16[64,4,6,128]{3,1,2,0:T(4,128)(2,1)}), bf16[64,4,6,128]{3,1,2,0:T(4,128)(2,1)S(1)}, u32[]{:S(2)}, u32[]{:S(2)}) %all-to-all-start) | async-done | bytes 393248 | tf_op jit(solution)/shard_map/all_to_all | solution.py:66
  186.1 0.8 copy.55
  (25 shorter events, 1.6 us)
Async XLA Ops:
  0.6 5.9 %copy-start.1 = (bf16[100,4,18,384]{3,1,2,0:T(4,128)(2,1)S(1)}, bf16[100,4,18,384]{3,1,2,0:T(4,128)(2,1)}, u32[]{:S(2)}) copy-start(bf16[100,4,18,384]{3,1,2,0:T(4,128)(2,1)} %param.7) | copy-start | bytes 16588804
  6.6 4.3 %copy-start.2 = (bf16[50,4,18,384]{3,1,2,0:T(4,128)(2,1)S(1)}, bf16[50,4,18,384]{3,1,2,0:T(4,128)(2,1)}, u32[]{:S(2)}) copy-start(bf16[50,4,18,384]{3,1,2,0:T(4,128)(2,1)} %param.6) | copy-start | bytes 8294404
  19.8 90.4 %copy-start.5 = (f32[100]{0:T(128)S(1)}, f32[100]{0:T(128)}, u32[]{:S(2)}) copy-start(f32[100]{0:T(128)} %param.8) | copy-start | bytes 1204
  115.9 12.0 %copy-start.3 = (s32[6,768]{1,0:T(8,128)S(1)}, s32[6,768]{1,0:T(8,128)}, u32[]{:S(2)}) copy-start(s32[6,768]{1,0:T(8,128)} %param.9) | copy-start | bytes 55300
  119.3 16.6 %copy-start = (bf16[50,4,18,384]{3,2,1,0:T(8,128)(2,1)S(1)}, bf16[50,4,18,384]{3,2,1,0:T(8,128)(2,1)}, u32[]{:S(2)}) copy-start(bf16[50,4,18,384]{3,2,1,0:T(8,128)(2,1)} %reshape.69) | copy-start | bytes 8294404
  122.3 8.8 %collective-permute-start = (bf16[50,4,3,384]{3,1,2,0:T(4,128)(2,1)S(1)}, bf16[50,4,3,384]{3,1,2,0:T(4,128)(2,1)S(1)}, u32[]{:S(2)}, u32[]{:S(2)}) collective-permute-start(bf16[50,4,3,384]{3,1,2,0:T(4,128)(2,1)S(1)} %copy.47), channel_id=1, source_target_pairs={{0,4},{4,8},{8,12},{12,16},{16,20},{20,24},{24,28},{28,32},{32,36}... | collective-permute-start | bytes 1382408 | tf_op jit(solution)/shard_map/ppermute | solution.py:14
  125.9 9.8 %collective-permute-start.1 = (bf16[50,4,3,384]{3,1,2,0:T(4,128)(2,1)S(1)}, bf16[50,4,3,384]{3,1,2,0:T(4,128)(2,1)S(1)}, u32[]{:S(2)}, u32[]{:S(2)}) collective-permute-start(bf16[50,4,3,384]{3,1,2,0:T(4,128)(2,1)S(1)} %copy.48), channel_id=1, source_target_pairs={{4,0},{8,4},{12,8},{16,12},{20,16},{24,20},{28,24},{32,28},{36,32}... | collective-permute-start | bytes 1382408 | tf_op jit(solution)/shard_map/ppermute | solution.py:17
  147.6 12.9 %copy-start.4 = (f32[6,768]{1,0:T(8,128)S(1)}, f32[6,768]{1,0:T(8,128)}, u32[]{:S(2)}) copy-start(f32[6,768]{1,0:T(8,128)} %param.10) | copy-start | bytes 55300
  147.6 14.9 %copy-start.6 = (s32[50]{0:T(128)S(1)}, s32[50]{0:T(128)}, u32[]{:S(2)}) copy-start(s32[50]{0:T(128)} %param.11) | copy-start | bytes 604
  164.1 22.0 %all-to-all-start = ((bf16[64,4,6,128]{3,1,2,0:T(4,128)(2,1)}), bf16[64,4,6,128]{3,1,2,0:T(4,128)(2,1)S(1)}, u32[]{:S(2)}, u32[]{:S(2)}) async-start(bf16[64,4,6,128]{3,1,2,0:T(4,128)(2,1)} %copy.53), calls=%async_computation | async-start | bytes 786432 | tf_op jit(solution)/shard_map/all_to_all | solution.py:66
where the time goes:
time: 188 us; the launch traced here: 187 us
  blocking collectives  81.6 us (43%)
  local copies, waits for them, and re-layouts  61.8 us (33%)
  waiting for transfers between devices  17.3 us (9%)
  starting transfers between devices  12.9 us (7%)
  matrix products  8.04 us (4%)
  other arithmetic  4.48 us (2%)
    psum x1, blocking collectives, shards(): projection = lax.psum(partial_sum, ('tile', 'lev'))  81.6 us
    gather x1, local copies, waits for them, and re-layouts, stencil_sums(): jnp.take(flat_pad, index_rows.reshape(-1), axis=1)  12.8 us
    convert_element_type x2, local copies, waits for them, and re-layouts, apply_update(): return (flat_x - increment).astype(jnp.bfloat16)  12.8 us
    unnamed x19, local copies, waits for them, and re-layouts  12.4 us
    all_to_all x1, waiting for transfers between devices, shards(): lax.all_to_all(outgoing, 'tile', split_axis=0, concat_axis=2, tiled=True)  9.96 us
    reshape x1, local copies, waits for them, and re-layouts, shards(): flat_v = lanczos.reshape(vectors, -1)  8.82 us
    all_to_all x1, starting transfers between devices, shards(): lax.all_to_all(outgoing, 'tile', split_axis=0, concat_axis=2, tiled=True)  7.38 us
    reshape x1, local copies, waits for them, and re-layouts, shards(): flat_pad = padded.reshape(members * levels, -1)  6.31 us
  transfers between devices with their start and end apart: 3, of which 3 were waited for; matrix products, arithmetic and copies ran while one was open for 3% of the time, Pallas kernels for 0%

commit v1 on v0

v1 whole, which is shorter than its diff:
```python
import functools
import math

import jax
import jax.numpy as jnp
from jax import lax
from jax.experimental import pallas as pl
from jax.experimental.pallas import tpu as pltpu
from jax.sharding import PartitionSpec as P

BF = jnp.bfloat16
F32 = jnp.float32
I32 = jnp.int32
MESH = pl.DeviceIdType.MESH

MEMBERS, VECTORS, LEV, ROWS, COLS = 50, 100, 4, 18, 384
POINTS, CELLS = 6, 768
HALO = 3
CB = COLS // 128
OWN = ROWS * CB
SIDE = HALO * CB
NB = OWN + 2 * SIDE
ML, KL = MEMBERS * LEV, VECTORS * LEV
SLOTS = 64
WAVES = 3
PM, PK = 64, 128


def iota(shape, dim):
    return lax.broadcasted_iota(I32, shape, dim)


def dot(a, b):
    return lax.dot_general(a, b, (((1,), (0,)), ((), ())), preferred_element_type=F32)


def one_hot(cond):
    return jnp.where(cond, 1.0, 0.0).astype(BF)


def split3(a):
    hi = a.astype(BF)
    rest = a - hi.astype(F32)
    mid = rest.astype(BF)
    return hi, mid, (rest - mid.astype(F32)).astype(BF)


def lanes(ref, first, count):
    return jnp.concatenate([ref[first + i] for i in range(count)], axis=1)


def prepare_stencil(idx, wgt, off, blk, wts):
    rows = [idx[p : p + 1, :] for p in range(POINTS)]
    weights = [wgt[p : p + 1, :] for p in range(POINTS)]
    for p in range(POINTS):
        moved = None
        for q in range(p + 1, POINTS):
            same = rows[p] == rows[q]
            hit = same if moved is None else same & ~moved
            weights[q] = jnp.where(hit, weights[q] + weights[p], weights[q])
            moved = same if moved is None else moved | same
        block = rows[p] >> 7
        blk[p : p + 1, :] = block if moved is None else jnp.where(moved, -1, block)
        off[p : p + 1, :] = rows[p] & 127
        wts[p : p + 1, :] = weights[p]


def build_stencil(off, blk, wts, sten, first, last):
    for c in range(CELLS // 128):
        cs = slice(c * 128, (c + 1) * 128)
        weights = [jnp.broadcast_to(wts[p : p + 1, cs], (16, 128)).astype(BF) for p in range(POINTS)]
        places = [(iota((16, 128), 0) + 16 * i).astype(F32).astype(BF) for i in range(8)]
        blocks, offsets = blk[:, cs], off[:, cs]

        def body(b, carry):
            local = jnp.where(blocks == b, offsets, -1).astype(F32)
            here = [jnp.broadcast_to(local[p : p + 1, :], (16, 128)).astype(BF) for p in range(POINTS)]
            for i in range(8):
                value = jnp.zeros((16, 128), BF)
                for p in range(POINTS):
                    value = jnp.where(here[p] == places[i], weights[p], value)
                sten[b, i * 16 : (i + 1) * 16, cs] = value
            return carry

        lax.fori_loop(first, last, body, 0)


def kernel(
    tiles, levs, g1, cells_total,
    x, v, idx, wgt, eig, slot,
    upd, own,
    xs, vs, us, lo, hi, sten, acc, off, blk, wts, part, ra, rb, rc, mine, ms,
    load_sem, out_sem, ar_send, ar_recv, halo_send, halo_recv, a2a_send, a2a_recv, self_sem,
):
    tile, lev = lax.axis_index("tile"), lax.axis_index("lev")
    g2t = tiles // g1
    g2 = g2t * levs
    member1 = lax.rem(tile, g1)
    group1 = tile // g1
    member2 = group1 * levs + lev

    chunks = 3
    per = ROWS // chunks

    def load_row(r, carry):
        k = r // per
        for c in range(CB):
            cols = pl.ds(c * 128, 128)
            pltpu.make_async_copy(x.at[:, r, :, cols], xs.at[r * CB + c], load_sem.at[k]).start()
            pltpu.make_async_copy(v.at[:, r, :, cols], vs.at[r * CB + c], load_sem.at[chunks + k]).start()
        return carry

    lax.fori_loop(0, ROWS, load_row, 0)

    barrier = pltpu.get_barrier_semaphore()

    def greet(d, carry):
        pl.semaphore_signal(
            barrier, inc=1, device_id={"tile": lax.rem(tile + d, tiles)}, device_id_type=MESH
        )
        return carry

    lax.fori_loop(1, tiles, greet, 0)

    def greet_lev(d, carry):
        e, q = d // g2t + 1, lax.rem(d, g2t)
        pl.semaphore_signal(
            barrier, inc=1,
            device_id={"tile": q * g1 + member1, "lev": lax.rem(lev + e, levs)},
            device_id_type=MESH,
        )
        return carry

    lax.fori_loop(0, (levs - 1) * g2t, greet_lev, 0)

    prepare_stencil(idx, wgt, off, blk, wts)
    build_stencil(off, blk, wts, sten, 0, NB)

    xf = xs.reshape(OWN, ML, 128)
    vf = vs.reshape(OWN, KL, 128)
    uf = us.reshape(OWN, ML, 128)
    step = OWN // chunks
    gram = None
    for k in range(chunks):
        here = pl.ds(k * step, step)
        pltpu.make_async_copy(xs.at[here], xs.at[here], load_sem.at[k]).wait()
        pltpu.make_async_copy(vs.at[here], vs.at[here], load_sem.at[chunks + k]).wait()
        term = lax.dot_general(
            lanes(xf, k * step, step), lanes(vf, k * step, step),
            (((1,), (1,)), ((), ())), preferred_element_type=F32,
        )
        gram = term if gram is None else gram + term
    same_lev = (iota((ML, KL), 0) & 3) == (iota((ML, KL), 1) & 3)
    gram = jnp.where(same_lev, gram, 0.0)
    fold_m = one_hot((iota((PM, ML), 1) >> 2) == iota((PM, ML), 0))
    fold_k = one_hot((iota((KL, PK), 0) >> 2) == iota((KL, PK), 1))
    folded = sum(dot(fold_m, piece) for piece in split3(gram))
    partial = sum(dot(piece, fold_k) for piece in split3(folded))
    sh = PM // g1
    part.reshape(PM, PK)[...] = partial

    pl.semaphore_wait(barrier, tiles - 1 + (levs - 1) * g2t)

    def send_a(d, carry):
        to = lax.rem(member1 + d, g1)
        pltpu.make_async_remote_copy(
            src_ref=part.at[to], dst_ref=ra.at[member1], send_sem=ar_send.at[0], recv_sem=ar_recv.at[0],
            device_id={"tile": group1 * g1 + to}, device_id_type=MESH,
        ).start()
        return carry

    lax.fori_loop(1, g1, send_a, 0)
    ra[member1] = part[member1]
    pltpu.make_async_copy(ra.at[pl.ds(0, g1 - 1)], ra.at[pl.ds(0, g1 - 1)], ar_recv.at[0]).wait()
    total = ra[0]
    for i in range(1, g1):
        total = total + ra[i]
    mine[0] = total

    def send_b(d, carry):
        to = lax.rem(member2 + d, g2)
        pltpu.make_async_remote_copy(
            src_ref=mine.at[0], dst_ref=rb.at[member2], send_sem=ar_send.at[1], recv_sem=ar_recv.at[1],
            device_id={"tile": (to // levs) * g1 + member1, "lev": lax.rem(to, levs)}, device_id_type=MESH,
        ).start()
        return carry

    lax.fori_loop(1, g2, send_b, 0)
    rb[member2] = total
    pltpu.make_async_copy(rb.at[pl.ds(0, g2 - 1)], rb.at[pl.ds(0, g2 - 1)], ar_recv.at[1]).wait()
    total = rb[0]
    for i in range(1, g2):
        total = total + rb[i]
    mine[1] = total

    def send_c(d, carry):
        to = lax.rem(member1 + d, g1)
        pltpu.make_async_remote_copy(
            src_ref=mine.at[1], dst_ref=rc.at[member1], send_sem=ar_send.at[2], recv_sem=ar_recv.at[2],
            device_id={"tile": group1 * g1 + to}, device_id_type=MESH,
        ).start()
        return carry

    lax.fori_loop(1, g1, send_c, 0)
    rc[member1] = total

    spread_m = one_hot((iota((ML, PM), 0) >> 2) == iota((ML, PM), 1))
    spread_k = one_hot((iota((PK, KL), 1) >> 2) == iota((PK, KL), 0))
    slot_row = jnp.broadcast_to(slot[...], (8, MEMBERS)).astype(F32).astype(BF)
    spread_slot = one_hot((iota((MEMBERS, ML), 1) >> 2) == iota((MEMBERS, ML), 0))
    slot_ml = dot(slot_row, spread_slot)[0:1, :].astype(I32)
    out_rows = SLOTS * LEV * 2
    row, col = iota((out_rows, ML), 0), iota((out_rows, ML), 1)
    taken = ((row >> 3) == slot_ml) & (((row >> 1) & 3) == (col & 3))
    select = [one_hot(taken & ((row & 1) == r)) for r in range(2)]

    pltpu.make_async_copy(rc.at[pl.ds(0, g1 - 1)], rc.at[pl.ds(0, g1 - 1)], ar_recv.at[2]).wait()
    projection = rc.reshape(PM, PK)[...]
    eig_row = jnp.concatenate([eig[...], jnp.zeros((1, PK - VECTORS), F32)], axis=1)
    coef = (eig_row * projection / math.sqrt(cells_total)).astype(BF)
    coef = dot(dot(spread_m, coef).astype(BF), spread_k)
    coef = jnp.where(same_lev, coef, 0.0).astype(BF)

    def update(first, count):
        inc = dot(coef, lanes(vf, first, count))
        for i in range(count):
            uf[first + i] = (
                xf[first + i].astype(F32) - inc[:, i * 128 : (i + 1) * 128]
            ).astype(BF)

    def halo_copy(first, dst, k, to):
        return pltpu.make_async_remote_copy(
            src_ref=us.at[pl.ds(first, SIDE)], dst_ref=dst, send_sem=halo_send.at[k],
            recv_sem=halo_recv.at[k], device_id={"tile": to}, device_id_type=MESH,
        )

    to_low = halo_copy(0, hi, 0, lax.rem(tile + tiles - 1, tiles))
    to_high = halo_copy(OWN - SIDE, lo, 1, lax.rem(tile + 1, tiles))
    update(0, SIDE)
    pl.when(tile > 0)(lambda: to_low.start())
    update(OWN - SIDE, SIDE)
    pl.when(tile < tiles - 1)(lambda: to_high.start())
    for i in range(2):
        update(SIDE + 18 * i, 18)

    def store_row(r, carry):
        for c in range(CB):
            pltpu.make_async_copy(us.at[r * CB + c], upd.at[:, r, :, pl.ds(c * 128, 128)], out_sem).start()
        return carry

    lax.fori_loop(0, ROWS, store_row, 0)

    acc[...] = dot(lanes(uf, 0, OWN), sten[pl.ds(SIDE, OWN)].reshape(OWN * 128, CELLS))

    @pl.when(tile == 0)
    def _():
        lo[...] = jnp.zeros_like(lo)

    @pl.when(tile == tiles - 1)
    def _():
        hi[...] = jnp.zeros_like(hi)

    pl.when(tile < tiles - 1)(lambda: to_low.wait_recv())
    pl.when(tile > 0)(lambda: to_high.wait_recv())

    wave_cells = CELLS // WAVES
    both = jnp.concatenate(
        [lanes(lo.reshape(SIDE, ML, 128), 0, SIDE), lanes(hi.reshape(SIDE, ML, 128), 0, SIDE)], axis=1
    )
    msf = ms.reshape(WAVES, out_rows, 128)
    for j in range(WAVES):
        cs = slice(j * wave_cells, (j + 1) * wave_cells)
        edge = jnp.concatenate(
            [
                sten[pl.ds(0, SIDE), :, cs].reshape(SIDE * 128, wave_cells),
                sten[pl.ds(SIDE + OWN, SIDE), :, cs].reshape(SIDE * 128, wave_cells),
            ],
            axis=0,
        )
        res = (acc[:, cs] + dot(both, edge)).astype(BF)
        msf[j] = (dot(select[0], res[:, :128]) + dot(select[1], res[:, 128:])).astype(BF)

        def send(d, carry):
            to = lax.rem(tile + d, tiles)
            pltpu.make_async_remote_copy(
                src_ref=ms.at[j, to], dst_ref=own.at[:, tile * WAVES + j], send_sem=a2a_send.at[j],
                recv_sem=a2a_recv, device_id={"tile": to}, device_id_type=MESH,
            ).start()
            return carry

        lax.fori_loop(1, tiles, send, 0)
        pltpu.make_async_copy(ms.at[j, tile], own.at[:, tile * WAVES + j], self_sem.at[j]).start()

    for k, n in ((0, g1), (1, g2), (2, g1)):
        pltpu.make_async_copy(ra.at[pl.ds(0, n - 1)], ra.at[pl.ds(0, n - 1)], ar_send.at[k]).wait()
    pl.when(tile > 0)(lambda: to_low.wait_send())
    pl.when(tile < tiles - 1)(lambda: to_high.wait_send())
    pltpu.make_async_copy(us, us, out_sem).wait()
    for j in range(WAVES):
        pltpu.make_async_copy(ms.at[j, tile], own.at[:, tile * WAVES + j], self_sem.at[j]).wait()
        others = ms.at[j, pl.ds(0, tiles - 1)]
        pltpu.make_async_copy(others, others, a2a_send.at[j]).wait()
    others = own.at[:, pl.ds(0, (tiles - 1) * WAVES)]
    pltpu.make_async_copy(others, others, a2a_recv).wait()


def shards(anomalies, lanczos, eigen_weight, stencil_index, stencil_weight, member_slot):
    tiles, levs = lax.axis_size("tile"), lax.axis_size("lev")
    g1 = min(16, tiles)
    g2 = tiles // g1 * levs
    sh = PM // g1
    total = LEV * ROWS * COLS * tiles * levs
    hbm = pl.BlockSpec(memory_space=pltpu.HBM)
    vmem = pl.BlockSpec(memory_space=pltpu.VMEM)
    updated, owned = pl.pallas_call(
        functools.partial(kernel, tiles, levs, g1, total),
        out_shape=(
            jax.ShapeDtypeStruct((MEMBERS, ROWS, LEV, COLS), BF),
            jax.ShapeDtypeStruct((LEV, tiles * WAVES, 2, 128), BF),
        ),
        in_specs=[hbm, hbm, vmem, vmem, vmem, vmem],
        out_specs=(hbm, hbm),
        scratch_shapes=[
            pltpu.VMEM((OWN, MEMBERS, LEV, 128), BF),
            pltpu.VMEM((OWN, VECTORS, LEV, 128), BF),
            pltpu.VMEM((OWN, MEMBERS, LEV, 128), BF),
            pltpu.VMEM((SIDE, MEMBERS, LEV, 128), BF),
            pltpu.VMEM((SIDE, MEMBERS, LEV, 128), BF),
            pltpu.VMEM((NB, 128, CELLS), BF),
            pltpu.VMEM((ML, CELLS), F32),
            pltpu.VMEM((POINTS, CELLS), I32),
            pltpu.VMEM((POINTS, CELLS), I32),
            pltpu.VMEM((POINTS, CELLS), F32),
            pltpu.VMEM((g1, sh, PK), F32),
            pltpu.VMEM((g1, sh, PK), F32),
            pltpu.VMEM((g2, sh, PK), F32),
            pltpu.VMEM((g1, sh, PK), F32),
            pltpu.VMEM((2, sh, PK), F32),
            pltpu.VMEM((WAVES, SLOTS, LEV, 2, 128), BF),
            pltpu.SemaphoreType.DMA((6,)),
            pltpu.SemaphoreType.DMA(()),
            pltpu.SemaphoreType.DMA((3,)),
            pltpu.SemaphoreType.DMA((3,)),
            pltpu.SemaphoreType.DMA((2,)),
            pltpu.SemaphoreType.DMA((2,)),
            pltpu.SemaphoreType.DMA((WAVES,)),
            pltpu.SemaphoreType.DMA(()),
            pltpu.SemaphoreType.DMA((WAVES,)),
        ],
        compiler_params=pltpu.CompilerParams(
            collective_id=0, has_side_effects=True, vmem_limit_bytes=56 * 2**20
        ),
    )(
        anomalies.transpose(0, 2, 1, 3),
        lanczos.transpose(0, 2, 1, 3),
        stencil_index,
        stencil_weight,
        eigen_weight.reshape(1, -1),
        member_slot.reshape(1, -1),
    )
    return updated.transpose(0, 2, 1, 3), owned.reshape(1, LEV, tiles * 6, 128)


def solution(mesh):
    placed = (
        P(None, "lev", "tile", None),
        P(None, "lev", "tile", None),
        P(),
        P(None, "tile"),
        P(None, "tile"),
        P(),
    )
    return jax.shard_map(
        shards,
        mesh=mesh,
        in_specs=placed,
        out_specs=(P(None, "lev", "tile", None), P("tile", "lev", None, None)),
        check_vma=False,
    )
```

time: 188 us -> 65 us (0.35)
  blocking collectives: 81.6 us -> 0 us
  Pallas kernels: 0 us -> 59.2 us
  local copies, waits for them, and re-layouts: 61.8 us -> 5.07 us
  waiting for transfers between devices: 17.3 us -> 0 us
  starting transfers between devices: 12.9 us -> 0 us
  matrix products: 8.04 us -> 0 us
  other arithmetic: 4.48 us -> 0 us
    psum x1 -> x0, blocking collectives: 81.6 us -> none  [shards(): projection = lax.psum(partial_sum, ('tile', 'lev'))]
    pallas_call x0 -> x1, Pallas kernels: none -> 59.2 us  [shards(): pl.pallas_call(functools.partial(kernel, tiles, levs, g1, total), out_sha...]
    reshape x5 -> x0, local copies, waits for them, and re-layouts: 19.9 us -> none  [the longest x1 8.82 us: shards(): flat_v = lanczos.reshape(vectors, -1)]
    convert_element_type x3 -> x0, local copies, waits for them, and re-layouts: 13 us -> none  [the longest x2 12.8 us: apply_update(): return (flat_x - increment).astype(jnp.bfloat16)]
    gather x1 -> x0, local copies, waits for them, and re-layouts: 12.8 us -> none  [stencil_sums(): jnp.take(flat_pad, index_rows.reshape(-1), axis=1)]
    all_to_all x1 -> x0, waiting for transfers between devices: 9.96 us -> none  [shards(): lax.all_to_all(outgoing, 'tile', split_axis=0, concat_axis=2, tiled=True)]
    dot_general x3 -> x0, matrix products: 8.04 us -> none  [the longest x1 5.69 us: apply_update(): lax.dot_general(coefficients, flat_v, (((0,), (0,)), ((), ())), preferred...]
    all_to_all x1 -> x0, starting transfers between devices: 7.38 us -> none  [shards(): lax.all_to_all(outgoing, 'tile', split_axis=0, concat_axis=2, tiled=True)]
  transfers between devices with their start and end apart: 3 -> 0, of which waited for: 3 -> 0; matrix products, arithmetic and copies ran while one was open for 3% -> 0% of each run, Pallas kernels for 0% -> 0%
where the time goes in v1:
time: 65 us; the launch traced here: 64.9 us
  Pallas kernels  59.2 us (91%)
  local copies, waits for them, and re-layouts  5.07 us (8%)
  between operations  0.65 us (1%)
    pallas_call x1, Pallas kernels, shards(): pl.pallas_call(functools.partial(kernel, tiles, levs, g1, total), out_sha...  59.2 us
    unnamed x4, local copies, waits for them, and re-layouts  5.07 us

profile of v1, /device:TPU:1, one launch (start us, length us, event | category | flops | bytes accessed | tf_op | source)
XLA Modules:
  0.0 64.9 jit_solution(15324480979847914777)
XLA Ops:
  0.6 59.2 %shard_map.77 = (bf16[50,18,4,384]{3,2,1,0:T(4,128)(2,1)}, bf16[4,192,2,128]{3,2,1,0:T(2,128)(2,1)}) custom-call(bf16[50,18,4,384]{3,2,1,0:T(4,128)(2,1)} %bitcast.7, bf16[100,18,4,384]{3,2,1,0:T(4,128)(2,1)} %bitcast.6, s32[6,768]{1,0:T(8,128)} %idx.1, f32[6,768]{1,0:T(8,128)} %wgt.1, f32[1,100]{1,0:T(1,128)} %bitcast.10, s32[1,50]{1,0:T(1,128)} %bitcast.11), custom_call_target="tpu_custom_call" | custom-call | tf_op jit(solution)/shard_map/pallas_call | solution.py:315
  59.8 0.0 copy-start
  59.8 4.3 %copy.10 = bf16[50,4,18,384]{3,1,2,0:T(4,128)(2,1)} copy(bf16[50,4,18,384]{3,1,2,0:T(4,128)(2,1)} %bitcast.8) | data formatting | bytes 5529600
  64.1 0.0 copy-done
  64.1 0.7 %copy.11 = bf16[1,4,384,128]{3,2,1,0:T(8,128)(2,1)} copy(bf16[1,4,384,128]{3,2,1,0:T(8,128)(2,1)S(1)} %bitcast.9) | data formatting | bytes 786432
Async XLA Ops:
  59.8 4.3 %copy-start = (bf16[4,192,2,128]{3,2,1,0:T(2,128)(2,1)S(1)}, bf16[4,192,2,128]{3,2,1,0:T(2,128)(2,1)}, u32[]{:S(2)}) copy-start(bf16[4,192,2,128]{3,2,1,0:T(2,128)(2,1)} %get-tuple-element.5) | copy-start | bytes 1179652

commit v2 on v1

--- a/solution.py
+++ b/solution.py
@@ -23,6 +23,7 @@
 ML, KL = MEMBERS * LEV, VECTORS * LEV
 SLOTS = 64
 WAVES = 3
+BUILD = ((0, 10), (10, 15), (15, 20), (20, 46), (46, NB))
 PM, PK = 64, 128
 
 
@@ -47,6 +48,11 @@
 
 def lanes(ref, first, count):
     return jnp.concatenate([ref[first + i] for i in range(count)], axis=1)
+
+
+def far_first(i, n):
+    half, sign = (i + 1) // 2, 1 - 2 * lax.rem(i, 2)
+    return lax.rem(n // 2 + sign * half + n, n)
 
 
 def prepare_stencil(idx, wgt, off, blk, wts):
@@ -86,18 +92,35 @@
 
 
 def kernel(
-    tiles, levs, g1, cells_total,
-    x, v, idx, wgt, eig, slot,
+    tiles, levs, grid, cells_total,
+    x, v, idx_in, wgt_in, eig_in, slot_in,
     upd, own,
-    xs, vs, us, lo, hi, sten, acc, off, blk, wts, part, ra, rb, rc, mine, ms,
+    idx, wgt, eig, slot, small_sem, xs, vs, us, lo, hi, sten, acc, off, blk, wts, part, ra, rb, rc, sums, ms,
     load_sem, out_sem, ar_send, ar_recv, halo_send, halo_recv, a2a_send, a2a_recv, self_sem,
 ):
     tile, lev = lax.axis_index("tile"), lax.axis_index("lev")
-    g2t = tiles // g1
-    g2 = g2t * levs
-    member1 = lax.rem(tile, g1)
-    group1 = tile // g1
-    member2 = group1 * levs + lev
+    nx, nz, nc = grid
+    row_len = nz * nc
+    my_x, my_zc = tile // row_len, lax.rem(tile, row_len)
+    my_z, my_c = my_zc // nc, lax.rem(my_zc, nc)
+    n1, n2 = nx * levs, nz * nc
+    mine1, mine2 = my_x * levs + lev, my_zc
+
+    def peer1(i):
+        to_x = lax.rem(my_x + far_first(i // levs, nx), nx)
+        to_lev = lax.rem(lev + far_first(lax.rem(i, levs), levs), levs)
+        return to_x * levs + to_lev, {"tile": to_x * row_len + my_zc, "lev": to_lev}
+
+    def peer2(i):
+        to_z = lax.rem(my_z + far_first(i // nc, nz), nz)
+        to_c = lax.rem(my_c + far_first(lax.rem(i, nc), nc), nc)
+        return to_z * nc + to_c, {"tile": my_x * row_len + to_z * nc + to_c}
+
+    def peer_tile(i):
+        to_z = lax.rem(my_z + far_first(i // (nx * nc), nz), nz)
+        to_x = lax.rem(my_x + far_first(lax.rem(i // nc, nx), nx), nx)
+        to_c = lax.rem(my_c + far_first(lax.rem(i, nc), nc), nc)
+        return to_x * row_len + to_z * nc + to_c
 
     chunks = 3
     per = ROWS // chunks
@@ -110,31 +133,35 @@
             pltpu.make_async_copy(v.at[:, r, :, cols], vs.at[r * CB + c], load_sem.at[chunks + k]).start()
         return carry
 
+    smalls = [
+        pltpu.make_async_copy(src, dst, small_sem.at[i])
+        for i, (src, dst) in enumerate(((idx_in, idx), (wgt_in, wgt), (eig_in, eig), (slot_in, slot)))
+    ]
+    for copy in smalls:
+        copy.start()
     lax.fori_loop(0, ROWS, load_row, 0)
 
     barrier = pltpu.get_barrier_semaphore()
 
-    def greet(d, carry):
-        pl.semaphore_signal(
-            barrier, inc=1, device_id={"tile": lax.rem(tile + d, tiles)}, device_id_type=MESH
-        )
+    def greet(i, carry):
+        pl.semaphore_signal(barrier, inc=1, device_id={"tile": peer_tile(i)}, device_id_type=MESH)
         return carry
 
-    lax.fori_loop(1, tiles, greet, 0)
-
-    def greet_lev(d, carry):
-        e, q = d // g2t + 1, lax.rem(d, g2t)
-        pl.semaphore_signal(
-            barrier, inc=1,
-            device_id={"tile": q * g1 + member1, "lev": lax.rem(lev + e, levs)},
-            device_id_type=MESH,
-        )
+    def greet_lev(i, carry):
+        to = {
+            "tile": i // (levs - 1) * row_len + my_zc,
+            "lev": lax.rem(lev + 1 + lax.rem(i, levs - 1), levs),
+        }
+        pl.semaphore_signal(barrier, inc=1, device_id=to, device_id_type=MESH)
         return carry
 
-    lax.fori_loop(0, (levs - 1) * g2t, greet_lev, 0)
-
+    lax.fori_loop(0, tiles - 1, greet, 0)
+    if levs > 1:
+        lax.fori_loop(0, nx * (levs - 1), greet_lev, 0)
+
+    for copy in smalls:
+        copy.wait()
     prepare_stencil(idx, wgt, off, blk, wts)
-    build_stencil(off, blk, wts, sten, 0, NB)
 
     xf = xs.reshape(OWN, ML, 128)
     vf = vs.reshape(OWN, KL, 128)
@@ -142,6 +169,7 @@
     step = OWN // chunks
     gram = None
     for k in range(chunks):
+        build_stencil(off, blk, wts, sten, *BUILD[k])
         here = pl.ds(k * step, step)
         pltpu.make_async_copy(xs.at[here], xs.at[here], load_sem.at[k]).wait()
         pltpu.make_async_copy(vs.at[here], vs.at[here], load_sem.at[chunks + k]).wait()
@@ -156,53 +184,45 @@
     fold_k = one_hot((iota((KL, PK), 0) >> 2) == iota((KL, PK), 1))
     folded = sum(dot(fold_m, piece) for piece in split3(gram))
     partial = sum(dot(piece, fold_k) for piece in split3(folded))
-    sh = PM // g1
     part.reshape(PM, PK)[...] = partial
 
-    pl.semaphore_wait(barrier, tiles - 1 + (levs - 1) * g2t)
-
-    def send_a(d, carry):
-        to = lax.rem(member1 + d, g1)
-        pltpu.make_async_remote_copy(
-            src_ref=part.at[to], dst_ref=ra.at[member1], send_sem=ar_send.at[0], recv_sem=ar_recv.at[0],
-            device_id={"tile": group1 * g1 + to}, device_id_type=MESH,
-        ).start()
-        return carry
-
-    lax.fori_loop(1, g1, send_a, 0)
-    ra[member1] = part[member1]
-    pltpu.make_async_copy(ra.at[pl.ds(0, g1 - 1)], ra.at[pl.ds(0, g1 - 1)], ar_recv.at[0]).wait()
-    total = ra[0]
-    for i in range(1, g1):
-        total = total + ra[i]
-    mine[0] = total
-
-    def send_b(d, carry):
-        to = lax.rem(member2 + d, g2)
-        pltpu.make_async_remote_copy(
-            src_ref=mine.at[0], dst_ref=rb.at[member2], send_sem=ar_send.at[1], recv_sem=ar_recv.at[1],
-            device_id={"tile": (to // levs) * g1 + member1, "lev": lax.rem(to, levs)}, device_id_type=MESH,
-        ).start()
-        return carry
-
-    lax.fori_loop(1, g2, send_b, 0)
-    rb[member2] = total
-    pltpu.make_async_copy(rb.at[pl.ds(0, g2 - 1)], rb.at[pl.ds(0, g2 - 1)], ar_recv.at[1]).wait()
-    total = rb[0]
-    for i in range(1, g2):
-        total = total + rb[i]
-    mine[1] = total
-
-    def send_c(d, carry):
-        to = lax.rem(member1 + d, g1)
-        pltpu.make_async_remote_copy(
-            src_ref=mine.at[1], dst_ref=rc.at[member1], send_sem=ar_send.at[2], recv_sem=ar_recv.at[2],
-            device_id={"tile": group1 * g1 + to}, device_id_type=MESH,
-        ).start()
-        return carry
-
-    lax.fori_loop(1, g1, send_c, 0)
-    rc[member1] = total
+    pl.semaphore_wait(barrier, tiles - 1 + nx * (levs - 1))
+
+    def ar_stage(k, n, peer, src, dst, mine):
+        def send(i, carry):
+            to, device = peer(i)
+            pltpu.make_async_remote_copy(
+                src_ref=src(to), dst_ref=dst.at[mine], send_sem=ar_send.at[k], recv_sem=ar_recv.at[k],
+                device_id=device, device_id_type=MESH,
+            ).start()
+            return carry
+
+        lax.fori_loop(0, n - 1, send, 0)
+
+    def ar_wait(k, n, dst):
+        got = dst.at[pl.ds(0, n - 1)]
+        pltpu.make_async_copy(got, got, ar_recv.at[k]).wait()
+
+    def add_up(ref, n):
+        terms = [ref[i] for i in range(n)]
+        while len(terms) > 1:
+            terms = [a + b for a, b in zip(terms[::2], terms[1::2])]
+        return terms[0]
+
+    ar_stage(0, n1, peer1, lambda to: part.at[to], ra, mine1)
+    ra[mine1] = part[mine1]
+    build_stencil(off, blk, wts, sten, *BUILD[3])
+    ar_wait(0, n1, ra)
+    total = add_up(ra, n1)
+    sums[0] = total
+    ar_stage(1, n2, peer2, lambda to: sums.at[0], rb, mine2)
+    rb[mine2] = total
+    build_stencil(off, blk, wts, sten, *BUILD[4])
+    ar_wait(1, n2, rb)
+    total = add_up(rb, n2)
+    sums[1] = total
+    ar_stage(2, n1, peer1, lambda to: sums.at[1], rc, mine1)
+    rc[mine1] = total
 
     spread_m = one_hot((iota((ML, PM), 0) >> 2) == iota((ML, PM), 1))
     spread_k = one_hot((iota((PK, KL), 1) >> 2) == iota((PK, KL), 0))
@@ -214,7 +234,7 @@
     taken = ((row >> 3) == slot_ml) & (((row >> 1) & 3) == (col & 3))
     select = [one_hot(taken & ((row & 1) == r)) for r in range(2)]
 
-    pltpu.make_async_copy(rc.at[pl.ds(0, g1 - 1)], rc.at[pl.ds(0, g1 - 1)], ar_recv.at[2]).wait()
+    ar_wait(2, n1, rc)
     projection = rc.reshape(PM, PK)[...]
     eig_row = jnp.concatenate([eig[...], jnp.zeros((1, PK - VECTORS), F32)], axis=1)
     coef = (eig_row * projection / math.sqrt(cells_total)).astype(BF)
@@ -280,19 +300,20 @@
         res = (acc[:, cs] + dot(both, edge)).astype(BF)
         msf[j] = (dot(select[0], res[:, :128]) + dot(select[1], res[:, 128:])).astype(BF)
 
-        def send(d, carry):
-            to = lax.rem(tile + d, tiles)
+        def send(i, carry):
+            to = peer_tile(i)
             pltpu.make_async_remote_copy(
                 src_ref=ms.at[j, to], dst_ref=own.at[:, tile * WAVES + j], send_sem=a2a_send.at[j],
                 recv_sem=a2a_recv, device_id={"tile": to}, device_id_type=MESH,
             ).start()
             return carry
 
-        lax.fori_loop(1, tiles, send, 0)
+        lax.fori_loop(0, tiles - 1, send, 0)
         pltpu.make_async_copy(ms.at[j, tile], own.at[:, tile * WAVES + j], self_sem.at[j]).start()
 
-    for k, n in ((0, g1), (1, g2), (2, g1)):
-        pltpu.make_async_copy(ra.at[pl.ds(0, n - 1)], ra.at[pl.ds(0, n - 1)], ar_send.at[k]).wait()
+    for k, n, dst in ((0, n1, ra), (1, n2, rb), (2, n1, rc)):
+        sent = dst.at[pl.ds(0, n - 1)]
+        pltpu.make_async_copy(sent, sent, ar_send.at[k]).wait()
     pl.when(tile > 0)(lambda: to_low.wait_send())
     pl.when(tile < tiles - 1)(lambda: to_high.wait_send())
     pltpu.make_async_copy(us, us, out_sem).wait()
@@ -304,23 +325,37 @@
     pltpu.make_async_copy(others, others, a2a_recv).wait()
 
 
+def deliver(a, b, upd, own, sem):
+    copies = [pltpu.make_async_copy(a, upd, sem.at[0]), pltpu.make_async_copy(b, own, sem.at[1])]
+    for copy in copies:
+        copy.start()
+    for copy in copies:
+        copy.wait()
+
+
 def shards(anomalies, lanczos, eigen_weight, stencil_index, stencil_weight, member_slot):
     tiles, levs = lax.axis_size("tile"), lax.axis_size("lev")
-    g1 = min(16, tiles)
-    g2 = tiles // g1 * levs
-    sh = PM // g1
+    grid = (4, 8, 2) if tiles == 64 else (1, 1, tiles)
+    n1, n2 = grid[0] * levs, grid[1] * grid[2]
+    sh = PM // n1
     total = LEV * ROWS * COLS * tiles * levs
     hbm = pl.BlockSpec(memory_space=pltpu.HBM)
-    vmem = pl.BlockSpec(memory_space=pltpu.VMEM)
+    shapes = (
+        jax.ShapeDtypeStruct((MEMBERS, ROWS, LEV, COLS), BF),
+        jax.ShapeDtypeStruct((LEV, tiles * WAVES, 2, 128), BF),
+    )
+    anywhere = pl.BlockSpec(memory_space=pl.ANY)
     updated, owned = pl.pallas_call(
-        functools.partial(kernel, tiles, levs, g1, total),
-        out_shape=(
-            jax.ShapeDtypeStruct((MEMBERS, ROWS, LEV, COLS), BF),
-            jax.ShapeDtypeStruct((LEV, tiles * WAVES, 2, 128), BF),
-        ),
-        in_specs=[hbm, hbm, vmem, vmem, vmem, vmem],
-        out_specs=(hbm, hbm),
+        functools.partial(kernel, tiles, levs, grid, total),
+        out_shape=shapes,
+        in_specs=[hbm] * 6,
+        out_specs=(anywhere, anywhere),
         scratch_shapes=[
+            pltpu.VMEM((POINTS, CELLS), I32),
+            pltpu.VMEM((POINTS, CELLS), F32),
+            pltpu.VMEM((1, VECTORS), F32),
+            pltpu.VMEM((1, MEMBERS), I32),
+            pltpu.SemaphoreType.DMA((4,)),
             pltpu.VMEM((OWN, MEMBERS, LEV, 128), BF),
             pltpu.VMEM((OWN, VECTORS, LEV, 128), BF),
             pltpu.VMEM((OWN, MEMBERS, LEV, 128), BF),
@@ -331,10 +366,10 @@
             pltpu.VMEM((POINTS, CELLS), I32),
             pltpu.VMEM((POINTS, CELLS), I32),
             pltpu.VMEM((POINTS, CELLS), F32),
-            pltpu.VMEM((g1, sh, PK), F32),
-            pltpu.VMEM((g1, sh, PK), F32),
-            pltpu.VMEM((g2, sh, PK), F32),
-            pltpu.VMEM((g1, sh, PK), F32),
+            pltpu.VMEM((n1, sh, PK), F32),
+            pltpu.VMEM((n1, sh, PK), F32),
+            pltpu.VMEM((n2, sh, PK), F32),
+            pltpu.VMEM((n1, sh, PK), F32),
             pltpu.VMEM((2, sh, PK), F32),
             pltpu.VMEM((WAVES, SLOTS, LEV, 2, 128), BF),
             pltpu.SemaphoreType.DMA((6,)),
@@ -348,16 +383,29 @@
             pltpu.SemaphoreType.DMA((WAVES,)),
         ],
         compiler_params=pltpu.CompilerParams(
-            collective_id=0, has_side_effects=True, vmem_limit_bytes=56 * 2**20
+            collective_id=0, has_side_effects=True, vmem_limit_bytes=36 * 2**20
         ),
     )(
-        anomalies.transpose(0, 2, 1, 3),
-        lanczos.transpose(0, 2, 1, 3),
-        stencil_index,
-        stencil_weight,
-        eigen_weight.reshape(1, -1),
-        member_slot.reshape(1, -1),
+        *(
+            pltpu.with_memory_space_constraint(a, pltpu.HBM)
+            for a in (
+                anomalies.transpose(0, 2, 1, 3),
+                lanczos.transpose(0, 2, 1, 3),
+                stencil_index,
+                stencil_weight,
+                eigen_weight.reshape(1, -1),
+                member_slot.reshape(1, -1),
+            )
+        )
     )
+    updated, owned = pl.pallas_call(
+        deliver,
+        out_shape=shapes,
+        in_specs=[anywhere, anywhere],
+        out_specs=(hbm, hbm),
+        scratch_shapes=[pltpu.SemaphoreType.DMA((2,))],
+        compiler_params=pltpu.CompilerParams(vmem_limit_bytes=2**20),
+    )(updated, owned)
     return updated.transpose(0, 2, 1, 3), owned.reshape(1, LEV, tiles * 6, 128)
 
 

time: 65 us -> 59.7 us (0.918)
  local copies, waits for them, and re-layouts: 5.07 us -> 0 us
    unnamed x4 -> x0, local copies, waits for them, and re-layouts: 5.07 us -> none
    pallas_call x1 -> x2, Pallas kernels: 59.2 us -> 58.9 us  [the longest x1 57.3 us: shards(): pl.pallas_call(functools.partial(kernel, tiles, levs, grid, total), out_s...]
where the time goes in v2:
time: 59.7 us; the launch traced here: 59.6 us
  Pallas kernels  58.9 us (99%)
  between operations  0.64 us (1%)
    pallas_call x1, Pallas kernels, shards(): pl.pallas_call(functools.partial(kernel, tiles, levs, grid, total), out_s...  57.3 us
    pallas_call x1, Pallas kernels, shards(): pl.pallas_call(deliver, out_shape=shapes, in_specs=[anywhere, anywhere],...  1.68 us

profile of v2, /device:TPU:1, one launch (start us, length us, event | category | flops | bytes accessed | tf_op | source)
XLA Modules:
  0.0 59.6 jit_solution(14238494357042384265)
XLA Ops:
  0.6 57.3 %shard_map.77 = (bf16[50,18,4,384]{3,2,1,0:T(4,128)(2,1)S(1)}, bf16[4,192,2,128]{3,2,1,0:T(2,128)(2,1)S(1)}) custom-call(bf16[50,18,4,384]{3,2,1,0:T(4,128)(2,1)} %bitcast.7, bf16[100,18,4,384]{3,2,1,0:T(4,128)(2,1)} %bitcast.6, s32[6,768]{1,0:T(8,128)} %idx_in.1, f32[6,768]{1,0:T(8,128)} %wgt_in.1, f32[1,100]{1,0:T(1,128)} %bitcast.8, s32[1,50]{1,0:T(1,128)} %bitcast.9), custom_call_target="tpu_custom_call" | custom-call | tf_op jit(solution)/shard_map/pallas_call | solution.py:348
  57.9 1.7 %shard_map.78 = (bf16[50,18,4,384]{3,2,1,0:T(4,128)(2,1)}, bf16[4,192,2,128]{3,2,1,0:T(2,128)(2,1)}) custom-call(bf16[50,18,4,384]{3,2,1,0:T(4,128)(2,1)S(1)} %get-tuple-element.6.a, bf16[4,192,2,128]{3,2,1,0:T(2,128)(2,1)S(1)} %get-tuple-element.7.b), custom_call_target="tpu_custom_call" | custom-call | tf_op jit(solution)/shard_map/pallas_call | solution.py:401

commit v3 on v2

--- a/solution.py
+++ b/solution.py
@@ -95,7 +95,7 @@
     tiles, levs, grid, cells_total,
     x, v, idx_in, wgt_in, eig_in, slot_in,
     upd, own,
-    idx, wgt, eig, slot, small_sem, xs, vs, us, lo, hi, sten, acc, off, blk, wts, part, ra, rb, rc, sums, ms,
+    idx, wgt, eig, slot, small_sem, xs, vs, us, sten, off, blk, wts, part, ra, rb, rc, sums, ms,
     load_sem, out_sem, ar_send, ar_recv, halo_send, halo_recv, a2a_send, a2a_recv, self_sem,
 ):
     tile, lev = lax.axis_index("tile"), lax.axis_index("lev")
@@ -129,8 +129,9 @@
         k = r // per
         for c in range(CB):
             cols = pl.ds(c * 128, 128)
-            pltpu.make_async_copy(x.at[:, r, :, cols], xs.at[r * CB + c], load_sem.at[k]).start()
-            pltpu.make_async_copy(v.at[:, r, :, cols], vs.at[r * CB + c], load_sem.at[chunks + k]).start()
+            b = SIDE + r * CB + c
+            pltpu.make_async_copy(x.at[:, r, :, cols], xs.at[b], load_sem.at[k]).start()
+            pltpu.make_async_copy(v.at[:, r, :, cols], vs.at[b], load_sem.at[chunks + k]).start()
         return carry
 
     smalls = [
@@ -163,18 +164,19 @@
         copy.wait()
     prepare_stencil(idx, wgt, off, blk, wts)
 
-    xf = xs.reshape(OWN, ML, 128)
-    vf = vs.reshape(OWN, KL, 128)
-    uf = us.reshape(OWN, ML, 128)
+    xf = xs.reshape(NB, ML, 128)
+    vf = vs.reshape(NB, KL, 128)
+    uf = us.reshape(NB, ML, 128)
     step = OWN // chunks
     gram = None
     for k in range(chunks):
         build_stencil(off, blk, wts, sten, *BUILD[k])
-        here = pl.ds(k * step, step)
+        first = SIDE + k * step
+        here = pl.ds(first, step)
         pltpu.make_async_copy(xs.at[here], xs.at[here], load_sem.at[k]).wait()
         pltpu.make_async_copy(vs.at[here], vs.at[here], load_sem.at[chunks + k]).wait()
         term = lax.dot_general(
-            lanes(xf, k * step, step), lanes(vf, k * step, step),
+            lanes(xf, first, step), lanes(vf, first, step),
             (((1,), (1,)), ((), ())), preferred_element_type=F32,
         )
         gram = term if gram is None else gram + term
@@ -187,6 +189,36 @@
     part.reshape(PM, PK)[...] = partial
 
     pl.semaphore_wait(barrier, tiles - 1 + nx * (levs - 1))
+
+    def halo_copy(ref, first, dst, k, to):
+        return pltpu.make_async_remote_copy(
+            src_ref=ref.at[pl.ds(first, SIDE)], dst_ref=ref.at[pl.ds(dst, SIDE)], send_sem=halo_send.at[k],
+            recv_sem=halo_recv.at[k], device_id={"tile": to}, device_id_type=MESH,
+        )
+
+    down, up = lax.rem(tile + tiles - 1, tiles), lax.rem(tile + 1, tiles)
+    to_low = [halo_copy(ref, SIDE, SIDE + OWN, k, down) for k, ref in enumerate((xs, vs))]
+    to_high = [halo_copy(ref, OWN, 0, 2 + k, up) for k, ref in enumerate((xs, vs))]
+
+    @pl.when(tile > 0)
+    def _():
+        for copy in to_low:
+            copy.start()
+
+    @pl.when(tile < tiles - 1)
+    def _():
+        for copy in to_high:
+            copy.start()
+
+    @pl.when(tile == 0)
+    def _():
+        for ref in (xs, vs):
+            ref[pl.ds(0, SIDE)] = jnp.zeros((SIDE,) + ref.shape[1:], BF)
+
+    @pl.when(tile == tiles - 1)
+    def _():
+        for ref in (xs, vs):
+            ref[pl.ds(SIDE + OWN, SIDE)] = jnp.zeros((SIDE,) + ref.shape[1:], BF)
 
     def ar_stage(k, n, peer, src, dst, mine):
         def send(i, carry):
@@ -248,56 +280,36 @@
                 xf[first + i].astype(F32) - inc[:, i * 128 : (i + 1) * 128]
             ).astype(BF)
 
-    def halo_copy(first, dst, k, to):
-        return pltpu.make_async_remote_copy(
-            src_ref=us.at[pl.ds(first, SIDE)], dst_ref=dst, send_sem=halo_send.at[k],
-            recv_sem=halo_recv.at[k], device_id={"tile": to}, device_id_type=MESH,
-        )
-
-    to_low = halo_copy(0, hi, 0, lax.rem(tile + tiles - 1, tiles))
-    to_high = halo_copy(OWN - SIDE, lo, 1, lax.rem(tile + 1, tiles))
-    update(0, SIDE)
-    pl.when(tile > 0)(lambda: to_low.start())
-    update(OWN - SIDE, SIDE)
-    pl.when(tile < tiles - 1)(lambda: to_high.start())
-    for i in range(2):
-        update(SIDE + 18 * i, 18)
+    for i in range(chunks):
+        update(SIDE + step * i, step)
 
     def store_row(r, carry):
         for c in range(CB):
-            pltpu.make_async_copy(us.at[r * CB + c], upd.at[:, r, :, pl.ds(c * 128, 128)], out_sem).start()
+            pltpu.make_async_copy(
+                us.at[SIDE + r * CB + c], upd.at[:, r, :, pl.ds(c * 128, 128)], out_sem
+            ).start()
         return carry
 
     lax.fori_loop(0, ROWS, store_row, 0)
 
-    acc[...] = dot(lanes(uf, 0, OWN), sten[pl.ds(SIDE, OWN)].reshape(OWN * 128, CELLS))
-
-    @pl.when(tile == 0)
-    def _():
-        lo[...] = jnp.zeros_like(lo)
-
-    @pl.when(tile == tiles - 1)
-    def _():
-        hi[...] = jnp.zeros_like(hi)
-
-    pl.when(tile < tiles - 1)(lambda: to_low.wait_recv())
-    pl.when(tile > 0)(lambda: to_high.wait_recv())
+    @pl.when(tile < tiles - 1)
+    def _():
+        for copy in to_low:
+            copy.wait_recv()
+
+    @pl.when(tile > 0)
+    def _():
+        for copy in to_high:
+            copy.wait_recv()
+
+    update(0, SIDE)
+    update(SIDE + OWN, SIDE)
 
     wave_cells = CELLS // WAVES
-    both = jnp.concatenate(
-        [lanes(lo.reshape(SIDE, ML, 128), 0, SIDE), lanes(hi.reshape(SIDE, ML, 128), 0, SIDE)], axis=1
-    )
     msf = ms.reshape(WAVES, out_rows, 128)
     for j in range(WAVES):
         cs = slice(j * wave_cells, (j + 1) * wave_cells)
-        edge = jnp.concatenate(
-            [
-                sten[pl.ds(0, SIDE), :, cs].reshape(SIDE * 128, wave_cells),
-                sten[pl.ds(SIDE + OWN, SIDE), :, cs].reshape(SIDE * 128, wave_cells),
-            ],
-            axis=0,
-        )
-        res = (acc[:, cs] + dot(both, edge)).astype(BF)
+        res = dot(lanes(uf, 0, NB), sten[:, :, cs].reshape(NB * 128, wave_cells)).astype(BF)
         msf[j] = (dot(select[0], res[:, :128]) + dot(select[1], res[:, 128:])).astype(BF)
 
         def send(i, carry):
@@ -314,9 +326,19 @@
     for k, n, dst in ((0, n1, ra), (1, n2, rb), (2, n1, rc)):
         sent = dst.at[pl.ds(0, n - 1)]
         pltpu.make_async_copy(sent, sent, ar_send.at[k]).wait()
-    pl.when(tile > 0)(lambda: to_low.wait_send())
-    pl.when(tile < tiles - 1)(lambda: to_high.wait_send())
-    pltpu.make_async_copy(us, us, out_sem).wait()
+
+    @pl.when(tile > 0)
+    def _():
+        for copy in to_low:
+            copy.wait_send()
+
+    @pl.when(tile < tiles - 1)
+    def _():
+        for copy in to_high:
+            copy.wait_send()
+
+    stored = us.at[pl.ds(0, OWN)]
+    pltpu.make_async_copy(stored, stored, out_sem).wait()
     for j in range(WAVES):
         pltpu.make_async_copy(ms.at[j, tile], own.at[:, tile * WAVES + j], self_sem.at[j]).wait()
         others = ms.at[j, pl.ds(0, tiles - 1)]
@@ -356,13 +378,10 @@
             pltpu.VMEM((1, VECTORS), F32),
             pltpu.VMEM((1, MEMBERS), I32),
             pltpu.SemaphoreType.DMA((4,)),
-            pltpu.VMEM((OWN, MEMBERS, LEV, 128), BF),
-            pltpu.VMEM((OWN, VECTORS, LEV, 128), BF),
-            pltpu.VMEM((OWN, MEMBERS, LEV, 128), BF),
-            pltpu.VMEM((SIDE, MEMBERS, LEV, 128), BF),
-            pltpu.VMEM((SIDE, MEMBERS, LEV, 128), BF),
+            pltpu.VMEM((NB, MEMBERS, LEV, 128), BF),
+            pltpu.VMEM((NB, VECTORS, LEV, 128), BF),
+            pltpu.VMEM((NB, MEMBERS, LEV, 128), BF),
             pltpu.VMEM((NB, 128, CELLS), BF),
-            pltpu.VMEM((ML, CELLS), F32),
             pltpu.VMEM((POINTS, CELLS), I32),
             pltpu.VMEM((POINTS, CELLS), I32),
             pltpu.VMEM((POINTS, CELLS), F32),
@@ -376,14 +395,14 @@
             pltpu.SemaphoreType.DMA(()),
             pltpu.SemaphoreType.DMA((3,)),
             pltpu.SemaphoreType.DMA((3,)),
-            pltpu.SemaphoreType.DMA((2,)),
-            pltpu.SemaphoreType.DMA((2,)),
+            pltpu.SemaphoreType.DMA((4,)),
+            pltpu.SemaphoreType.DMA((4,)),
             pltpu.SemaphoreType.DMA((WAVES,)),
             pltpu.SemaphoreType.DMA(()),
             pltpu.SemaphoreType.DMA((WAVES,)),
         ],
         compiler_params=pltpu.CompilerParams(
-            collective_id=0, has_side_effects=True, vmem_limit_bytes=36 * 2**20
+            collective_id=0, has_side_effects=True, vmem_limit_bytes=40 * 2**20
         ),
     )(
         *(

time: 59.7 us -> 71.2 us (1.19)
  Pallas kernels: 58.9 us -> 70.4 us
    pallas_call x1, Pallas kernels: 57.3 us -> 68.7 us  [shards(): pl.pallas_call(functools.partial(kernel, tiles, levs, grid, total), out_s...]
where the time goes in v3:
time: 71.2 us
  Pallas kernels  70.4 us (99%)
  between operations  0.8 us (1%)
    pallas_call x1, Pallas kernels, shards(): pl.pallas_call(functools.partial(kernel, tiles, levs, grid, total), out_s...  68.7 us
    pallas_call x1, Pallas kernels, shards(): pl.pallas_call(deliver, out_shape=shapes, in_specs=[anywhere, anywhere],...  1.68 us

profile of v3, /device:TPU:1, one launch (start us, length us, event | category | flops | bytes accessed | tf_op | source)
XLA Modules:
  0.0 71.2 jit_solution(1144370123349664153)
XLA Ops:
  0.6 68.7 %shard_map.77 = (bf16[50,18,4,384]{3,2,1,0:T(4,128)(2,1)S(1)}, bf16[4,192,2,128]{3,2,1,0:T(2,128)(2,1)S(1)}) custom-call(bf16[50,18,4,384]{3,2,1,0:T(4,128)(2,1)} %bitcast.7, bf16[100,18,4,384]{3,2,1,0:T(4,128)(2,1)} %bitcast.6, s32[6,768]{1,0:T(8,128)} %idx_in.1, f32[6,768]{1,0:T(8,128)} %wgt_in.1, f32[1,100]{1,0:T(1,128)} %bitcast.8, s32[1,50]{1,0:T(1,128)} %bitcast.9), custom_call_target="tpu_custom_call" | custom-call | tf_op jit(solution)/shard_map/pallas_call | solution.py:370
  69.3 1.7 %shard_map.78 = (bf16[50,18,4,384]{3,2,1,0:T(4,128)(2,1)}, bf16[4,192,2,128]{3,2,1,0:T(2,128)(2,1)}) custom-call(bf16[50,18,4,384]{3,2,1,0:T(4,128)(2,1)S(1)} %get-tuple-element.6.a, bf16[4,192,2,128]{3,2,1,0:T(2,128)(2,1)S(1)} %get-tuple-element.7.b), custom_call_target="tpu_custom_call" | custom-call | tf_op jit(solution)/shard_map/pallas_call | solution.py:420

commit v4 on v2

--- a/solution.py
+++ b/solution.py
@@ -50,9 +50,8 @@
     return jnp.concatenate([ref[first + i] for i in range(count)], axis=1)
 
 
-def far_first(i, n):
-    half, sign = (i + 1) // 2, 1 - 2 * lax.rem(i, 2)
-    return lax.rem(n // 2 + sign * half + n, n)
+def far_first(i):
+    return ((((0x01627354 >> ((i >> 3) * 4)) & 7) << 1) | (((i >> 1) & 3) << 4) | (i & 1)) ^ 49
 
 
 def prepare_stencil(idx, wgt, off, blk, wts):
@@ -102,25 +101,16 @@
     nx, nz, nc = grid
     row_len = nz * nc
     my_x, my_zc = tile // row_len, lax.rem(tile, row_len)
-    my_z, my_c = my_zc // nc, lax.rem(my_zc, nc)
     n1, n2 = nx * levs, nz * nc
     mine1, mine2 = my_x * levs + lev, my_zc
+    lev_bits = levs.bit_length() - 1
 
     def peer1(i):
-        to_x = lax.rem(my_x + far_first(i // levs, nx), nx)
-        to_lev = lax.rem(lev + far_first(lax.rem(i, levs), levs), levs)
-        return to_x * levs + to_lev, {"tile": to_x * row_len + my_zc, "lev": to_lev}
+        to = mine1 ^ i
+        return to, {"tile": (to >> lev_bits) * row_len + my_zc, "lev": to & (levs - 1)}
 
     def peer2(i):
-        to_z = lax.rem(my_z + far_first(i // nc, nz), nz)
-        to_c = lax.rem(my_c + far_first(lax.rem(i, nc), nc), nc)
-        return to_z * nc + to_c, {"tile": my_x * row_len + to_z * nc + to_c}
-
-    def peer_tile(i):
-        to_z = lax.rem(my_z + far_first(i // (nx * nc), nz), nz)
-        to_x = lax.rem(my_x + far_first(lax.rem(i // nc, nx), nx), nx)
-        to_c = lax.rem(my_c + far_first(lax.rem(i, nc), nc), nc)
-        return to_x * row_len + to_z * nc + to_c
+        return mine2 ^ i, {"tile": tile ^ i}
 
     chunks = 3
     per = ROWS // chunks
@@ -144,20 +134,14 @@
     barrier = pltpu.get_barrier_semaphore()
 
     def greet(i, carry):
-        pl.semaphore_signal(barrier, inc=1, device_id={"tile": peer_tile(i)}, device_id_type=MESH)
+        pl.semaphore_signal(barrier, inc=1, device_id={"tile": tile ^ i}, device_id_type=MESH)
         return carry
 
-    def greet_lev(i, carry):
-        to = {
-            "tile": i // (levs - 1) * row_len + my_zc,
-            "lev": lax.rem(lev + 1 + lax.rem(i, levs - 1), levs),
-        }
-        pl.semaphore_signal(barrier, inc=1, device_id=to, device_id_type=MESH)
-        return carry
-
-    lax.fori_loop(0, tiles - 1, greet, 0)
-    if levs > 1:
-        lax.fori_loop(0, nx * (levs - 1), greet_lev, 0)
+    lax.fori_loop(1, tiles, greet, 0)
+    for e in range(1, levs):
+        for q in range(nx):
+            to = {"tile": tile ^ (q * row_len), "lev": lev ^ e}
+            pl.semaphore_signal(barrier, inc=1, device_id=to, device_id_type=MESH)
 
     for copy in smalls:
         copy.wait()
@@ -197,7 +181,7 @@
             ).start()
             return carry
 
-        lax.fori_loop(0, n - 1, send, 0)
+        lax.fori_loop(1, n, send, 0)
 
     def ar_wait(k, n, dst):
         got = dst.at[pl.ds(0, n - 1)]
@@ -287,7 +271,7 @@
     both = jnp.concatenate(
         [lanes(lo.reshape(SIDE, ML, 128), 0, SIDE), lanes(hi.reshape(SIDE, ML, 128), 0, SIDE)], axis=1
     )
-    msf = ms.reshape(WAVES, out_rows, 128)
+    msf = ms.reshape(SLOTS, WAVES, LEV * 2, 128)
     for j in range(WAVES):
         cs = slice(j * wave_cells, (j + 1) * wave_cells)
         edge = jnp.concatenate(
@@ -298,18 +282,20 @@
             axis=0,
         )
         res = (acc[:, cs] + dot(both, edge)).astype(BF)
-        msf[j] = (dot(select[0], res[:, :128]) + dot(select[1], res[:, 128:])).astype(BF)
-
-        def send(i, carry):
-            to = peer_tile(i)
-            pltpu.make_async_remote_copy(
-                src_ref=ms.at[j, to], dst_ref=own.at[:, tile * WAVES + j], send_sem=a2a_send.at[j],
-                recv_sem=a2a_recv, device_id={"tile": to}, device_id_type=MESH,
-            ).start()
-            return carry
-
-        lax.fori_loop(0, tiles - 1, send, 0)
-        pltpu.make_async_copy(ms.at[j, tile], own.at[:, tile * WAVES + j], self_sem.at[j]).start()
+        picked = dot(select[0], res[:, :128]) + dot(select[1], res[:, 128:])
+        msf[:, j] = picked.astype(BF).reshape(SLOTS, LEV * 2, 128)
+
+    def send(i, carry):
+        to = tile ^ far_first(i)
+        pltpu.make_async_remote_copy(
+            src_ref=ms.at[to], dst_ref=own.at[tile], send_sem=a2a_send, recv_sem=a2a_recv,
+            device_id={"tile": to}, device_id_type=MESH,
+        ).start()
+        return carry
+
+    lax.fori_loop(0, tiles - 1, send, 0)
+    keep = pltpu.make_async_copy(ms.at[tile], own.at[tile], self_sem)
+    keep.start()
 
     for k, n, dst in ((0, n1, ra), (1, n2, rb), (2, n1, rc)):
         sent = dst.at[pl.ds(0, n - 1)]
@@ -317,16 +303,19 @@
     pl.when(tile > 0)(lambda: to_low.wait_send())
     pl.when(tile < tiles - 1)(lambda: to_high.wait_send())
     pltpu.make_async_copy(us, us, out_sem).wait()
+    keep.wait()
+    if tiles > 1:
+        others = ms.at[pl.ds(0, tiles - 1)]
+        pltpu.make_async_copy(others, others, a2a_send).wait()
+        pltpu.make_async_copy(others, others, a2a_recv).wait()
+
+
+def deliver(a, b, upd, own, sem):
+    copies = [pltpu.make_async_copy(a, upd, sem.at[0])]
     for j in range(WAVES):
-        pltpu.make_async_copy(ms.at[j, tile], own.at[:, tile * WAVES + j], self_sem.at[j]).wait()
-        others = ms.at[j, pl.ds(0, tiles - 1)]
-        pltpu.make_async_copy(others, others, a2a_send.at[j]).wait()
-    others = own.at[:, pl.ds(0, (tiles - 1) * WAVES)]
-    pltpu.make_async_copy(others, others, a2a_recv).wait()
-
-
-def deliver(a, b, upd, own, sem):
-    copies = [pltpu.make_async_copy(a, upd, sem.at[0]), pltpu.make_async_copy(b, own, sem.at[1])]
+        for lev in range(LEV):
+            k = 1 + j * LEV + lev
+            copies.append(pltpu.make_async_copy(b.at[:, j, lev], own.at[lev, :, j], sem.at[k]))
     for copy in copies:
         copy.start()
     for copy in copies:
@@ -342,8 +331,9 @@
     hbm = pl.BlockSpec(memory_space=pltpu.HBM)
     shapes = (
         jax.ShapeDtypeStruct((MEMBERS, ROWS, LEV, COLS), BF),
-        jax.ShapeDtypeStruct((LEV, tiles * WAVES, 2, 128), BF),
+        jax.ShapeDtypeStruct((tiles, WAVES, LEV, 2, 128), BF),
     )
+    final = (shapes[0], jax.ShapeDtypeStruct((LEV, tiles, WAVES, 2, 128), BF))
     anywhere = pl.BlockSpec(memory_space=pl.ANY)
     updated, owned = pl.pallas_call(
         functools.partial(kernel, tiles, levs, grid, total),
@@ -371,16 +361,16 @@
             pltpu.VMEM((n2, sh, PK), F32),
             pltpu.VMEM((n1, sh, PK), F32),
             pltpu.VMEM((2, sh, PK), F32),
-            pltpu.VMEM((WAVES, SLOTS, LEV, 2, 128), BF),
+            pltpu.VMEM((SLOTS, WAVES, LEV, 2, 128), BF),
             pltpu.SemaphoreType.DMA((6,)),
             pltpu.SemaphoreType.DMA(()),
             pltpu.SemaphoreType.DMA((3,)),
             pltpu.SemaphoreType.DMA((3,)),
             pltpu.SemaphoreType.DMA((2,)),
             pltpu.SemaphoreType.DMA((2,)),
-            pltpu.SemaphoreType.DMA((WAVES,)),
             pltpu.SemaphoreType.DMA(()),
-            pltpu.SemaphoreType.DMA((WAVES,)),
+            pltpu.SemaphoreType.DMA(()),
+            pltpu.SemaphoreType.DMA(()),
         ],
         compiler_params=pltpu.CompilerParams(
             collective_id=0, has_side_effects=True, vmem_limit_bytes=36 * 2**20
@@ -400,10 +390,10 @@
     )
     updated, owned = pl.pallas_call(
         deliver,
-        out_shape=shapes,
+        out_shape=final,
         in_specs=[anywhere, anywhere],
         out_specs=(hbm, hbm),
-        scratch_shapes=[pltpu.SemaphoreType.DMA((2,))],
+        scratch_shapes=[pltpu.SemaphoreType.DMA((1 + WAVES * LEV,))],
         compiler_params=pltpu.CompilerParams(vmem_limit_bytes=2**20),
     )(updated, owned)
     return updated.transpose(0, 2, 1, 3), owned.reshape(1, LEV, tiles * 6, 128)

time: 59.7 us -> 54 us (0.905)
  Pallas kernels: 58.9 us -> 53.3 us
    pallas_call x1, Pallas kernels: 57.3 us -> 51.5 us  [shards(): pl.pallas_call(functools.partial(kernel, tiles, levs, grid, total), out_s...]
where the time goes in v4:
time: 54 us; the launch traced here: 53.9 us
  Pallas kernels  53.3 us (99%)
  between operations  0.64 us (1%)
    pallas_call x1, Pallas kernels, shards(): pl.pallas_call(functools.partial(kernel, tiles, levs, grid, total), out_s...  51.5 us
    pallas_call x1, Pallas kernels, shards(): pl.pallas_call(deliver, out_shape=final, in_specs=[anywhere, anywhere], o...  1.76 us

profile of v4, /device:TPU:1, one launch (start us, length us, event | category | flops | bytes accessed | tf_op | source)
XLA Modules:
  0.0 53.9 jit_solution(4740032461436163195)
XLA Ops:
  0.6 51.5 %shard_map.77 = (bf16[50,18,4,384]{3,2,1,0:T(4,128)(2,1)S(1)}, bf16[64,3,4,2,128]{4,3,2,1,0:T(2,128)(2,1)S(1)}) custom-call(bf16[50,18,4,384]{3,2,1,0:T(4,128)(2,1)} %bitcast.7, bf16[100,18,4,384]{3,2,1,0:T(4,128)(2,1)} %bitcast.6, s32[6,768]{1,0:T(8,128)} %idx_in.1, f32[6,768]{1,0:T(8,128)} %wgt_in.1, f32[1,100]{1,0:T(1,128)} %bitcast.8, s32[1,50]{1,0:T(1,128)} %bitcast.9), custom_call_target="tpu_custom_call" | custom-call | tf_op jit(solution)/shard_map/pallas_call | solution.py:338
  52.2 1.8 %shard_map.78 = (bf16[50,18,4,384]{3,2,1,0:T(4,128)(2,1)}, bf16[4,64,3,2,128]{4,3,2,1,0:T(2,128)(2,1)}) custom-call(bf16[50,18,4,384]{3,2,1,0:T(4,128)(2,1)S(1)} %get-tuple-element.6.a, bf16[64,3,4,2,128]{4,3,2,1,0:T(2,128)(2,1)S(1)} %get-tuple-element.7.b), custom_call_target="tpu_custom_call" | custom-call | tf_op jit(solution)/shard_map/pallas_call | solution.py:391

commit v5 on v4

--- a/solution.py
+++ b/solution.py
@@ -23,7 +23,7 @@
 ML, KL = MEMBERS * LEV, VECTORS * LEV
 SLOTS = 64
 WAVES = 3
-BUILD = ((0, 10), (10, 15), (15, 20), (20, 46), (46, NB))
+BUILD = ((9, 18), (18, 23), (23, 28), (28, 63))
 PM, PK = 64, 128
 
 
@@ -94,7 +94,7 @@
     tiles, levs, grid, cells_total,
     x, v, idx_in, wgt_in, eig_in, slot_in,
     upd, own,
-    idx, wgt, eig, slot, small_sem, xs, vs, us, lo, hi, sten, acc, off, blk, wts, part, ra, rb, rc, sums, ms,
+    idx, wgt, eig, slot, small_sem, xs, vs, us, lo, hi, sten, rx, rv, off, blk, wts, part, ra, rb, rc, sums, ms,
     load_sem, out_sem, ar_send, ar_recv, halo_send, halo_recv, a2a_send, a2a_recv, self_sem,
 ):
     tile, lev = lax.axis_index("tile"), lax.axis_index("lev")
@@ -193,6 +193,12 @@
             terms = [a + b for a, b in zip(terms[::2], terms[1::2])]
         return terms[0]
 
+    def restrict_inputs(first, last):
+        cs = slice(first, last)
+        matrix = sten[pl.ds(SIDE, OWN), :, cs].reshape(OWN * 128, last - first)
+        rx[:, cs] = dot(lanes(xf, 0, OWN), matrix)
+        rv[:, cs] = dot(lanes(vf, 0, OWN), matrix).astype(BF)
+
     ar_stage(0, n1, peer1, lambda to: part.at[to], ra, mine1)
     ra[mine1] = part[mine1]
     build_stencil(off, blk, wts, sten, *BUILD[3])
@@ -201,12 +207,13 @@
     sums[0] = total
     ar_stage(1, n2, peer2, lambda to: sums.at[0], rb, mine2)
     rb[mine2] = total
-    build_stencil(off, blk, wts, sten, *BUILD[4])
+    restrict_inputs(0, 512)
     ar_wait(1, n2, rb)
     total = add_up(rb, n2)
     sums[1] = total
     ar_stage(2, n1, peer1, lambda to: sums.at[1], rc, mine1)
     rc[mine1] = total
+    restrict_inputs(512, CELLS)
 
     spread_m = one_hot((iota((ML, PM), 0) >> 2) == iota((ML, PM), 1))
     spread_k = one_hot((iota((PK, KL), 1) >> 2) == iota((PK, KL), 0))
@@ -244,17 +251,11 @@
     pl.when(tile > 0)(lambda: to_low.start())
     update(OWN - SIDE, SIDE)
     pl.when(tile < tiles - 1)(lambda: to_high.start())
+    build_stencil(off, blk, wts, sten, 0, SIDE)
+    build_stencil(off, blk, wts, sten, SIDE + OWN, NB)
+    rx[...] = rx[...] - dot(coef, rv[...])
     for i in range(2):
         update(SIDE + 18 * i, 18)
-
-    def store_row(r, carry):
-        for c in range(CB):
-            pltpu.make_async_copy(us.at[r * CB + c], upd.at[:, r, :, pl.ds(c * 128, 128)], out_sem).start()
-        return carry
-
-    lax.fori_loop(0, ROWS, store_row, 0)
-
-    acc[...] = dot(lanes(uf, 0, OWN), sten[pl.ds(SIDE, OWN)].reshape(OWN * 128, CELLS))
 
     @pl.when(tile == 0)
     def _():
@@ -267,23 +268,25 @@
     pl.when(tile < tiles - 1)(lambda: to_low.wait_recv())
     pl.when(tile > 0)(lambda: to_high.wait_recv())
 
-    wave_cells = CELLS // WAVES
     both = jnp.concatenate(
         [lanes(lo.reshape(SIDE, ML, 128), 0, SIDE), lanes(hi.reshape(SIDE, ML, 128), 0, SIDE)], axis=1
     )
+    edge = jnp.concatenate(
+        [
+            sten[pl.ds(0, SIDE)].reshape(SIDE * 128, CELLS),
+            sten[pl.ds(SIDE + OWN, SIDE)].reshape(SIDE * 128, CELLS),
+        ],
+        axis=0,
+    )
+    res = (rx[...] + dot(both, edge)).astype(BF)
+
+    picked = sum(
+        dot(select[r], jnp.concatenate([res[:, k * 128 : k * 128 + 128] for k in range(r, 6, 2)], axis=1))
+        for r in range(2)
+    ).astype(BF)
     msf = ms.reshape(SLOTS, WAVES, LEV * 2, 128)
     for j in range(WAVES):
-        cs = slice(j * wave_cells, (j + 1) * wave_cells)
-        edge = jnp.concatenate(
-            [
-                sten[pl.ds(0, SIDE), :, cs].reshape(SIDE * 128, wave_cells),
-                sten[pl.ds(SIDE + OWN, SIDE), :, cs].reshape(SIDE * 128, wave_cells),
-            ],
-            axis=0,
-        )
-        res = (acc[:, cs] + dot(both, edge)).astype(BF)
-        picked = dot(select[0], res[:, :128]) + dot(select[1], res[:, 128:])
-        msf[:, j] = picked.astype(BF).reshape(SLOTS, LEV * 2, 128)
+        msf[:, j] = picked[:, j * 128 : (j + 1) * 128].reshape(SLOTS, LEV * 2, 128)
 
     def send(i, carry):
         to = tile ^ far_first(i)
@@ -296,6 +299,13 @@
     lax.fori_loop(0, tiles - 1, send, 0)
     keep = pltpu.make_async_copy(ms.at[tile], own.at[tile], self_sem)
     keep.start()
+
+    def store_row(r, carry):
+        for c in range(CB):
+            pltpu.make_async_copy(us.at[r * CB + c], upd.at[:, r, :, pl.ds(c * 128, 128)], out_sem).start()
+        return carry
+
+    lax.fori_loop(0, ROWS, store_row, 0)
 
     for k, n, dst in ((0, n1, ra), (1, n2, rb), (2, n1, rc)):
         sent = dst.at[pl.ds(0, n - 1)]
@@ -353,6 +363,7 @@
             pltpu.VMEM((SIDE, MEMBERS, LEV, 128), BF),
             pltpu.VMEM((NB, 128, CELLS), BF),
             pltpu.VMEM((ML, CELLS), F32),
+            pltpu.VMEM((KL, CELLS), BF),
             pltpu.VMEM((POINTS, CELLS), I32),
             pltpu.VMEM((POINTS, CELLS), I32),
             pltpu.VMEM((POINTS, CELLS), F32),
@@ -373,7 +384,7 @@
             pltpu.SemaphoreType.DMA(()),
         ],
         compiler_params=pltpu.CompilerParams(
-            collective_id=0, has_side_effects=True, vmem_limit_bytes=36 * 2**20
+            collective_id=0, has_side_effects=True, vmem_limit_bytes=40 * 2**20
         ),
     )(
         *(

time: 54 us -> 53.1 us (0.983)
  Pallas kernels: 53.3 us -> 52.3 us
    pallas_call x1, Pallas kernels: 51.5 us -> 50.5 us  [shards(): pl.pallas_call(functools.partial(kernel, tiles, levs, grid, total), out_s...]
where the time goes in v5:
time: 53.1 us
  Pallas kernels  52.3 us (98%)
  between operations  0.8 us (2%)
    pallas_call x1, Pallas kernels, shards(): pl.pallas_call(functools.partial(kernel, tiles, levs, grid, total), out_s...  50.5 us
    pallas_call x1, Pallas kernels, shards(): pl.pallas_call(deliver, out_shape=final, in_specs=[anywhere, anywhere], o...  1.76 us

profile of v5, /device:TPU:1, one launch (start us, length us, event | category | flops | bytes accessed | tf_op | source)
XLA Modules:
  0.0 53.1 jit_solution(18092720995194565141)
XLA Ops:
  0.6 50.5 %shard_map.77 = (bf16[50,18,4,384]{3,2,1,0:T(4,128)(2,1)S(1)}, bf16[64,3,4,2,128]{4,3,2,1,0:T(2,128)(2,1)S(1)}) custom-call(bf16[50,18,4,384]{3,2,1,0:T(4,128)(2,1)} %bitcast.7, bf16[100,18,4,384]{3,2,1,0:T(4,128)(2,1)} %bitcast.6, s32[6,768]{1,0:T(8,128)} %idx_in.1, f32[6,768]{1,0:T(8,128)} %wgt_in.1, f32[1,100]{1,0:T(1,128)} %bitcast.8, s32[1,50]{1,0:T(1,128)} %bitcast.9), custom_call_target="tpu_custom_call" | custom-call | tf_op jit(solution)/shard_map/pallas_call | solution.py:348
  51.1 1.8 %shard_map.78 = (bf16[50,18,4,384]{3,2,1,0:T(4,128)(2,1)}, bf16[4,64,3,2,128]{4,3,2,1,0:T(2,128)(2,1)}) custom-call(bf16[50,18,4,384]{3,2,1,0:T(4,128)(2,1)S(1)} %get-tuple-element.6.a, bf16[64,3,4,2,128]{4,3,2,1,0:T(2,128)(2,1)S(1)} %get-tuple-element.7.b), custom_call_target="tpu_custom_call" | custom-call | tf_op jit(solution)/shard_map/pallas_call | solution.py:402

commit v6 on v5

--- a/solution.py
+++ b/solution.py
@@ -23,7 +23,8 @@
 ML, KL = MEMBERS * LEV, VECTORS * LEV
 SLOTS = 64
 WAVES = 3
-BUILD = ((9, 18), (18, 23), (23, 28), (28, 63))
+BUILD = (9, 17, 21, 25, 63)
+EARLY = 512
 PM, PK = 64, 128
 
 
@@ -70,8 +71,8 @@
         wts[p : p + 1, :] = weights[p]
 
 
-def build_stencil(off, blk, wts, sten, first, last):
-    for c in range(CELLS // 128):
+def build_stencil(off, blk, wts, sten, first, last, low=0, high=CELLS):
+    for c in range(low // 128, high // 128):
         cs = slice(c * 128, (c + 1) * 128)
         weights = [jnp.broadcast_to(wts[p : p + 1, cs], (16, 128)).astype(BF) for p in range(POINTS)]
         places = [(iota((16, 128), 0) + 16 * i).astype(F32).astype(BF) for i in range(8)]
@@ -129,7 +130,8 @@
     ]
     for copy in smalls:
         copy.start()
-    lax.fori_loop(0, ROWS, load_row, 0)
+    for r in range(ROWS):
+        load_row(r, 0)
 
     barrier = pltpu.get_barrier_semaphore()
 
@@ -137,7 +139,8 @@
         pl.semaphore_signal(barrier, inc=1, device_id={"tile": tile ^ i}, device_id_type=MESH)
         return carry
 
-    lax.fori_loop(1, tiles, greet, 0)
+    for i in range(1, tiles):
+        greet(i, 0)
     for e in range(1, levs):
         for q in range(nx):
             to = {"tile": tile ^ (q * row_len), "lev": lev ^ e}
@@ -153,7 +156,7 @@
     step = OWN // chunks
     gram = None
     for k in range(chunks):
-        build_stencil(off, blk, wts, sten, *BUILD[k])
+        build_stencil(off, blk, wts, sten, BUILD[k], BUILD[k + 1], 0, EARLY)
         here = pl.ds(k * step, step)
         pltpu.make_async_copy(xs.at[here], xs.at[here], load_sem.at[k]).wait()
         pltpu.make_async_copy(vs.at[here], vs.at[here], load_sem.at[chunks + k]).wait()
@@ -181,7 +184,8 @@
             ).start()
             return carry
 
-        lax.fori_loop(1, n, send, 0)
+        for i in range(1, n):
+            send(i, 0)
 
     def ar_wait(k, n, dst):
         got = dst.at[pl.ds(0, n - 1)]
@@ -201,19 +205,20 @@
 
     ar_stage(0, n1, peer1, lambda to: part.at[to], ra, mine1)
     ra[mine1] = part[mine1]
-    build_stencil(off, blk, wts, sten, *BUILD[3])
+    build_stencil(off, blk, wts, sten, BUILD[3], BUILD[4], 0, EARLY)
     ar_wait(0, n1, ra)
     total = add_up(ra, n1)
     sums[0] = total
     ar_stage(1, n2, peer2, lambda to: sums.at[0], rb, mine2)
     rb[mine2] = total
-    restrict_inputs(0, 512)
+    restrict_inputs(0, EARLY)
     ar_wait(1, n2, rb)
     total = add_up(rb, n2)
     sums[1] = total
     ar_stage(2, n1, peer1, lambda to: sums.at[1], rc, mine1)
     rc[mine1] = total
-    restrict_inputs(512, CELLS)
+    build_stencil(off, blk, wts, sten, SIDE, SIDE + OWN, EARLY, CELLS)
+    build_stencil(off, blk, wts, sten, 0, SIDE, 0, EARLY)
 
     spread_m = one_hot((iota((ML, PM), 0) >> 2) == iota((ML, PM), 1))
     spread_k = one_hot((iota((PK, KL), 1) >> 2) == iota((PK, KL), 0))
@@ -251,11 +256,10 @@
     pl.when(tile > 0)(lambda: to_low.start())
     update(OWN - SIDE, SIDE)
     pl.when(tile < tiles - 1)(lambda: to_high.start())
-    build_stencil(off, blk, wts, sten, 0, SIDE)
+    restrict_inputs(EARLY, CELLS)
+    build_stencil(off, blk, wts, sten, 0, SIDE, EARLY, CELLS)
     build_stencil(off, blk, wts, sten, SIDE + OWN, NB)
     rx[...] = rx[...] - dot(coef, rv[...])
-    for i in range(2):
-        update(SIDE + 18 * i, 18)
 
     @pl.when(tile == 0)
     def _():
@@ -296,16 +300,21 @@
         ).start()
         return carry
 
-    lax.fori_loop(0, tiles - 1, send, 0)
+    for i in range(tiles - 1):
+        send(i, 0)
     keep = pltpu.make_async_copy(ms.at[tile], own.at[tile], self_sem)
     keep.start()
+
+    for i in range(2):
+        update(SIDE + 18 * i, 18)
 
     def store_row(r, carry):
         for c in range(CB):
             pltpu.make_async_copy(us.at[r * CB + c], upd.at[:, r, :, pl.ds(c * 128, 128)], out_sem).start()
         return carry
 
-    lax.fori_loop(0, ROWS, store_row, 0)
+    for r in range(ROWS):
+        store_row(r, 0)
 
     for k, n, dst in ((0, n1, ra), (1, n2, rb), (2, n1, rc)):
         sent = dst.at[pl.ds(0, n - 1)]

time: 53.1 us -> 54.6 us (1.028)
  Pallas kernels: 52.3 us -> 53.7 us
    pallas_call x1, Pallas kernels: 50.5 us -> 51.9 us  [shards(): pl.pallas_call(functools.partial(kernel, tiles, levs, grid, total), out_s...]
where the time goes in v6:
time: 54.6 us; the launch traced here: 54.5 us
  Pallas kernels  53.7 us (98%)
  between operations  0.8 us (1%)
    pallas_call x1, Pallas kernels, shards(): pl.pallas_call(functools.partial(kernel, tiles, levs, grid, total), out_s...  51.9 us
    pallas_call x1, Pallas kernels, shards(): pl.pallas_call(deliver, out_shape=final, in_specs=[anywhere, anywhere], o...  1.76 us

profile of v6, /device:TPU:1, one launch (start us, length us, event | category | flops | bytes accessed | tf_op | source)
XLA Modules:
  0.0 54.5 jit_solution(10885362775668190485)
XLA Ops:
  0.6 51.9 %shard_map.77 = (bf16[50,18,4,384]{3,2,1,0:T(4,128)(2,1)S(1)}, bf16[64,3,4,2,128]{4,3,2,1,0:T(2,128)(2,1)S(1)}) custom-call(bf16[50,18,4,384]{3,2,1,0:T(4,128)(2,1)} %bitcast.7, bf16[100,18,4,384]{3,2,1,0:T(4,128)(2,1)} %bitcast.6, s32[6,768]{1,0:T(8,128)} %idx_in.1, f32[6,768]{1,0:T(8,128)} %wgt_in.1, f32[1,100]{1,0:T(1,128)} %bitcast.8, s32[1,50]{1,0:T(1,128)} %bitcast.9), custom_call_target="tpu_custom_call" | custom-call | tf_op jit(solution)/shard_map/pallas_call | solution.py:357
  52.6 1.8 %shard_map.78 = (bf16[50,18,4,384]{3,2,1,0:T(4,128)(2,1)}, bf16[4,64,3,2,128]{4,3,2,1,0:T(2,128)(2,1)}) custom-call(bf16[50,18,4,384]{3,2,1,0:T(4,128)(2,1)S(1)} %get-tuple-element.6.a, bf16[64,3,4,2,128]{4,3,2,1,0:T(2,128)(2,1)S(1)} %get-tuple-element.7.b), custom_call_target="tpu_custom_call" | custom-call | tf_op jit(solution)/shard_map/pallas_call | solution.py:411

commit v7 on v6

--- a/solution.py
+++ b/solution.py
@@ -23,7 +23,7 @@
 ML, KL = MEMBERS * LEV, VECTORS * LEV
 SLOTS = 64
 WAVES = 3
-BUILD = (9, 17, 21, 25, 63)
+BUILD = (9, 18, 23, 28, 63)
 EARLY = 512
 PM, PK = 64, 128
 
@@ -130,8 +130,7 @@
     ]
     for copy in smalls:
         copy.start()
-    for r in range(ROWS):
-        load_row(r, 0)
+    lax.fori_loop(0, ROWS, load_row, 0)
 
     barrier = pltpu.get_barrier_semaphore()
 
@@ -139,8 +138,7 @@
         pl.semaphore_signal(barrier, inc=1, device_id={"tile": tile ^ i}, device_id_type=MESH)
         return carry
 
-    for i in range(1, tiles):
-        greet(i, 0)
+    lax.fori_loop(1, tiles, greet, 0)
     for e in range(1, levs):
         for q in range(nx):
             to = {"tile": tile ^ (q * row_len), "lev": lev ^ e}
@@ -184,8 +182,7 @@
             ).start()
             return carry
 
-        for i in range(1, n):
-            send(i, 0)
+        lax.fori_loop(1, n, send, 0)
 
     def ar_wait(k, n, dst):
         got = dst.at[pl.ds(0, n - 1)]
@@ -218,7 +215,7 @@
     ar_stage(2, n1, peer1, lambda to: sums.at[1], rc, mine1)
     rc[mine1] = total
     build_stencil(off, blk, wts, sten, SIDE, SIDE + OWN, EARLY, CELLS)
-    build_stencil(off, blk, wts, sten, 0, SIDE, 0, EARLY)
+    restrict_inputs(EARLY, CELLS)
 
     spread_m = one_hot((iota((ML, PM), 0) >> 2) == iota((ML, PM), 1))
     spread_k = one_hot((iota((PK, KL), 1) >> 2) == iota((PK, KL), 0))
@@ -256,8 +253,7 @@
     pl.when(tile > 0)(lambda: to_low.start())
     update(OWN - SIDE, SIDE)
     pl.when(tile < tiles - 1)(lambda: to_high.start())
-    restrict_inputs(EARLY, CELLS)
-    build_stencil(off, blk, wts, sten, 0, SIDE, EARLY, CELLS)
+    build_stencil(off, blk, wts, sten, 0, SIDE)
     build_stencil(off, blk, wts, sten, SIDE + OWN, NB)
     rx[...] = rx[...] - dot(coef, rv[...])
 
@@ -313,8 +309,7 @@
             pltpu.make_async_copy(us.at[r * CB + c], upd.at[:, r, :, pl.ds(c * 128, 128)], out_sem).start()
         return carry
 
-    for r in range(ROWS):
-        store_row(r, 0)
+    lax.fori_loop(0, ROWS, store_row, 0)
 
     for k, n, dst in ((0, n1, ra), (1, n2, rb), (2, n1, rc)):
         sent = dst.at[pl.ds(0, n - 1)]

time: 54.6 us -> 53.7 us (0.984)
  Pallas kernels: 53.7 us -> 52.9 us
    pallas_call x1, Pallas kernels: 51.9 us -> 51.1 us  [shards(): pl.pallas_call(functools.partial(kernel, tiles, levs, grid, total), out_s...]
where the time goes in v7:
time: 53.7 us
  Pallas kernels  52.9 us (99%)
  between operations  0.8 us (1%)
    pallas_call x1, Pallas kernels, shards(): pl.pallas_call(functools.partial(kernel, tiles, levs, grid, total), out_s...  51.1 us
    pallas_call x1, Pallas kernels, shards(): pl.pallas_call(deliver, out_shape=final, in_specs=[anywhere, anywhere], o...  1.76 us

profile of v7, /device:TPU:1, one launch (start us, length us, event | category | flops | bytes accessed | tf_op | source)
XLA Modules:
  0.0 53.7 jit_solution(13057982140836633186)
XLA Ops:
  0.6 51.1 %shard_map.77 = (bf16[50,18,4,384]{3,2,1,0:T(4,128)(2,1)S(1)}, bf16[64,3,4,2,128]{4,3,2,1,0:T(2,128)(2,1)S(1)}) custom-call(bf16[50,18,4,384]{3,2,1,0:T(4,128)(2,1)} %bitcast.7, bf16[100,18,4,384]{3,2,1,0:T(4,128)(2,1)} %bitcast.6, s32[6,768]{1,0:T(8,128)} %idx_in.1, f32[6,768]{1,0:T(8,128)} %wgt_in.1, f32[1,100]{1,0:T(1,128)} %bitcast.8, s32[1,50]{1,0:T(1,128)} %bitcast.9), custom_call_target="tpu_custom_call" | custom-call | tf_op jit(solution)/shard_map/pallas_call | solution.py:352
  51.7 1.8 %shard_map.78 = (bf16[50,18,4,384]{3,2,1,0:T(4,128)(2,1)}, bf16[4,64,3,2,128]{4,3,2,1,0:T(2,128)(2,1)}) custom-call(bf16[50,18,4,384]{3,2,1,0:T(4,128)(2,1)S(1)} %get-tuple-element.6.a, bf16[64,3,4,2,128]{4,3,2,1,0:T(2,128)(2,1)S(1)} %get-tuple-element.7.b), custom_call_target="tpu_custom_call" | custom-call | tf_op jit(solution)/shard_map/pallas_call | solution.py:406

commit v8 on v7

--- a/solution.py
+++ b/solution.py
@@ -130,19 +130,24 @@
     ]
     for copy in smalls:
         copy.start()
-    lax.fori_loop(0, ROWS, load_row, 0)
+    lax.fori_loop(0, per, load_row, 0)
 
     barrier = pltpu.get_barrier_semaphore()
 
     def greet(i, carry):
-        pl.semaphore_signal(barrier, inc=1, device_id={"tile": tile ^ i}, device_id_type=MESH)
+        pl.semaphore_signal(
+            barrier, inc=1, device_id={"tile": tile ^ far_first(i)}, device_id_type=MESH
+        )
         return carry
 
-    lax.fori_loop(1, tiles, greet, 0)
+    far = min(24, tiles - 1)
+    lax.fori_loop(0, far, greet, 0)
     for e in range(1, levs):
         for q in range(nx):
             to = {"tile": tile ^ (q * row_len), "lev": lev ^ e}
             pl.semaphore_signal(barrier, inc=1, device_id=to, device_id_type=MESH)
+    lax.fori_loop(per, ROWS, load_row, 0)
+    lax.fori_loop(far, tiles - 1, greet, 0)
 
     for copy in smalls:
         copy.wait()

time: 53.7 us -> 54.1 us (level)
  no operation moved by 1% of the time
where the time goes in v8:
time: 54.1 us; the launch traced here: 54 us
  Pallas kernels  53.2 us (98%)
  between operations  0.8 us (1%)
    pallas_call x1, Pallas kernels, shards(): pl.pallas_call(functools.partial(kernel, tiles, levs, grid, total), out_s...  51.4 us
    pallas_call x1, Pallas kernels, shards(): pl.pallas_call(deliver, out_shape=final, in_specs=[anywhere, anywhere], o...  1.76 us

profile of v8, /device:TPU:1, one launch (start us, length us, event | category | flops | bytes accessed | tf_op | source)
XLA Modules:
  0.0 54.0 jit_solution(14158478366597264759)
XLA Ops:
  0.6 51.4 %shard_map.77 = (bf16[50,18,4,384]{3,2,1,0:T(4,128)(2,1)S(1)}, bf16[64,3,4,2,128]{4,3,2,1,0:T(2,128)(2,1)S(1)}) custom-call(bf16[50,18,4,384]{3,2,1,0:T(4,128)(2,1)} %bitcast.7, bf16[100,18,4,384]{3,2,1,0:T(4,128)(2,1)} %bitcast.6, s32[6,768]{1,0:T(8,128)} %idx_in.1, f32[6,768]{1,0:T(8,128)} %wgt_in.1, f32[1,100]{1,0:T(1,128)} %bitcast.8, s32[1,50]{1,0:T(1,128)} %bitcast.9), custom_call_target="tpu_custom_call" | custom-call | tf_op jit(solution)/shard_map/pallas_call | solution.py:357
  52.1 1.8 %shard_map.78 = (bf16[50,18,4,384]{3,2,1,0:T(4,128)(2,1)}, bf16[4,64,3,2,128]{4,3,2,1,0:T(2,128)(2,1)}) custom-call(bf16[50,18,4,384]{3,2,1,0:T(4,128)(2,1)S(1)} %get-tuple-element.6.a, bf16[64,3,4,2,128]{4,3,2,1,0:T(2,128)(2,1)S(1)} %get-tuple-element.7.b), custom_call_target="tpu_custom_call" | custom-call | tf_op jit(solution)/shard_map/pallas_call | solution.py:411
